TPU v7x, 512 devices: a whole 4x4x16 slice. The times are simulated.
512 devices in a mesh: rows: 32 (over x, z_lo), chol: 16 (over z_hi, y, core).
Axes of the slice: x: 4, y: 4, z: 16 (z_hi: 2, z_lo: 8; z = z_hi * 8 + z_lo), core: 2. Of those that a mesh axis runs over, the one named last changes fastest.
Arguments:
- walkers: float32 [16, 1024, 128], P(None, 'rows'), may hold values from -9 to 9
- trial: float32 [1024, 128], replicated, may hold values from -0.2 to 0.2
- cholesky: float32 [256, 1048576], P('chol', 'rows'), may hold values from -0.25 to 0.25
- noise: float32 [16, 256], P(None, 'chol'), may hold values from -4 to 4
Outputs:
- propagated: float32 [16, 1024, 128], P('chol', 'rows')
- log_weight: float32 [16], replicated
All inputs are finite; a program needn't handle non-finite values.
Results may differ from a plain program's by a relative error of at most 0.00019.
Values sent between devices are 32-bit elements; how exact they have to be, the bound alone decides.
A program may use at most 64 MiB of HBM per device.

v0:
```python
import jax
import jax.numpy as jnp
from jax import lax
from jax.sharding import PartitionSpec as P

M = 1024
WALK_DEV = 1
TAYLOR = 6


def factor_solve(factor, right):
    middle = lax.linalg.triangular_solve(
        factor, right, left_side=True, lower=True, transpose_a=False
    )
    return lax.linalg.triangular_solve(factor, middle, left_side=True, lower=True, transpose_a=True)


def body(walkers, trial, cholesky, noise):
    high = lax.Precision.HIGHEST
    block = walkers.shape[1]
    row_start = lax.axis_index("rows") * block
    own_trial = lax.dynamic_slice_in_dim(trial, row_start, block, 0)
    partial_correlation = jnp.einsum("ia,wib->wab", own_trial, walkers, precision=high)
    correlation = lax.psum(partial_correlation, "rows")
    gram = jnp.einsum("wab,wac->wbc", correlation, correlation, precision=high)
    factor = jnp.linalg.cholesky(gram)
    right = jnp.einsum("wab,ka->wbk", correlation, trial, precision=high)
    inverse_trial = factor_solve(factor, right)
    green = jnp.einsum("wia,wak->wik", walkers, inverse_trial, precision=high)
    green = green.reshape(green.shape[0], block * M)
    partial_bias = 0.1 * lax.dot_general(
        green,
        cholesky,
        (((1,), (1,)), ((), ())),
        precision=high,
        preferred_element_type=jnp.float32,
    )
    bias = lax.psum(partial_bias, "rows")
    field = noise - bias
    log_weight = lax.psum(jnp.sum(field * bias - 0.5 * bias * bias, axis=1), "chol")
    walker_start = lax.axis_index("chol") * WALK_DEV
    summed = lax.psum(
        0.1 * jnp.dot(field, cholesky, precision=high, preferred_element_type=jnp.float32), "chol"
    )
    mine = lax.dynamic_slice_in_dim(summed, walker_start, WALK_DEV, 0)
    potential = mine.reshape(WALK_DEV, block, M)
    own_walkers = lax.dynamic_slice_in_dim(walkers, walker_start, WALK_DEV, 0)
    term = own_walkers
    propagated = own_walkers
    for order in range(1, TAYLOR + 1):
        term = jnp.einsum(
            "wik,wka->wia",
            potential,
            lax.all_gather(term, "rows", axis=1, tiled=True),
            precision=high,
        ) / float(order)
        propagated = propagated + term
    return (propagated, log_weight)


def solution(mesh):
    return jax.shard_map(
        body,
        mesh=mesh,
        in_specs=(P(None, "rows", None), P(), P("chol", "rows"), P(None, "chol")),
        out_specs=(P("chol", "rows", None), P()),
        check_vma=False,
    )
```

profile of v0, /device:TPU:24, one launch (start us, length us, event | category | flops | bytes accessed | tf_op | source)
XLA Modules:
  0.0 1859.7 jit_solution(9052972413298539374)
XLA Ops:
  7.2 0.0 copy-start
  7.2 0.0 all-reduce.3.cloned.1.call-start
  7.2 3.2 convolution_bitcast_fusion
  10.4 0.0 all-reduce.3.cloned.1.call-update
  10.4 0.0 all-reduce.5.cloned.1.call-start
  10.5 460.9 %all-reduce.3.cloned.1.call-done = f32[16,128,128]{2,1,0:T(8,128)} async-done(((f32[16,128,128]{2,1,0:T(8,128)}), f32[16,128,128]{2,1,0:T(8,128)}) %all-reduce.3.cloned.1.call-update) | async-done | bytes 1048592 | tf_op jit(solution)/shard_map/psum | solution.py:24
  471.5 3.4 fusion.17
  474.8 1.4 copy.9
  476.2 2.4 fusion.6
  478.6 0.0 copy-start.1
  478.6 189.1 %custom-call.9 = f32[16,128,128]{2,1,0:T(8,128)} custom-call(f32[16,128,128]{2,1,0:T(8,128)} %fusion.6), custom_call_target="Cholesky" | custom-call | tf_op jit(solution)/shard_map/jit(cholesky)/cholesky | solution.py:26
  667.7 1.3 select_reduce_fusion
  669.0 0.1 compare_reduce_fusion
  669.1 2.4 select_bitcast_fusion
  671.5 159.1 %custom-call.10 = f32[16,1,128,128]{2,3,1,0:T(8,128)} custom-call(f32[16,1,128,128]{3,2,1,0:T(8,128)} %select_bitcast_fusion), custom_call_target="InvertDiagBlocksLowerTriangular" | custom-call | tf_op jit(solution)/shard_map/triangular_solve | solution.py:15
  830.6 0.0 copy-done.1
  830.6 0.0 copy-start.2
  830.6 8.1 fusion.9
  838.7 0.0 copy-done.2
  838.7 8.6 fusion.4
  847.4 0.0 copy-start.3
  847.4 8.6 fusion.2
  856.0 0.0 copy-done.3
  856.0 4.7 fusion.18
  860.7 1.2 copy.11
  861.9 0.0 copy-done
  862.0 0.0 copy-start.4
  862.0 2.8 convolution_multiply_fusion.6
  864.8 124.8 %psum.29 = f32[16,16]{1,0:T(8,128)S(1)} all-reduce(f32[16,16]{1,0:T(8,128)S(1)} %convolution_multiply_fusion.6), channel_id=1, replica_groups=mesh['rows'=32,'chol'=16] {'rows'}, use_global_device_ids=true, to_apply=%region_3.4 | all-reduce | flops 256 | bytes 2048 | tf_op jit(solution)/shard_map/psum | solution.py:38
  989.6 0.0 copy-done.4
  989.6 3.2 convolution_multiply_fusion
  992.8 0.0 all-reduce.5.cloned.1.call-update
  992.9 127.4 %all_gather.18 = f32[1,1024,128]{2,1,0:T(8,128)S(1)} all-gather(f32[1,32,128]{2,1,0:T(8,128)S(1)} %constant_dynamic-slice_fusion), channel_id=1, replica_groups=mesh['rows'=32,'chol'=16] {'rows'}, dimensions={1}, use_global_device_ids=true | all-gather | bytes 540672 | tf_op jit(solution)/shard_map/all_gather | solution.py:54
  1120.3 0.1 fusion.14
  1120.4 49.8 %psum.31 = f32[16]{0:T(128)} all-reduce(f32[16]{0:T(128)S(1)} %fusion.14), channel_id=1, replica_groups=mesh['rows'=32,'chol'=16] {'chol'}, use_global_device_ids=true, to_apply=%region_6.7 | all-reduce | flops 16 | bytes 128 | tf_op jit(solution)/shard_map/psum | solution.py:40
  1170.2 88.9 %all-reduce.5.cloned.1.call-done = f32[16,32768]{1,0:T(8,128)} async-done(((f32[16,32768]{1,0:T(8,128)}), f32[16,32768]{1,0:T(8,128)}) %all-reduce.5.cloned.1.call-update) | async-done | bytes 2097168 | tf_op jit(solution)/shard_map/psum | solution.py:42
  1259.1 1.6 dynamic-slice_reduce_fusion
  1260.7 0.4 fusion.7
  1261.1 121.5 %all-gather = f32[1024,128]{1,0:T(8,128)S(1)} all-gather(f32[32,128]{1,0:T(8,128)S(1)} %fusion.7), channel_id=2, replica_groups=mesh['rows'=32,'chol'=16] {'rows'}, dimensions={0}, use_global_device_ids=true | all-gather | bytes 540672 | tf_op jit(solution)/shard_map/all_gather | solution.py:54
  1382.6 0.4 convolution_multiply_fusion.5
  1383.0 115.8 %all-gather.1 = f32[1024,128]{1,0:T(8,128)S(1)} all-gather(f32[32,128]{1,0:T(8,128)S(1)} %convolution_multiply_fusion.5), channel_id=3, replica_groups=mesh['rows'=32,'chol'=16] {'rows'}, dimensions={0}, use_global_device_ids=true | all-gather | bytes 540672 | tf_op jit(solution)/shard_map/all_gather | solution.py:54
  1498.8 0.4 convolution_multiply_fusion.4
  1499.2 117.8 %all-gather.2 = f32[1024,128]{1,0:T(8,128)S(1)} all-gather(f32[32,128]{1,0:T(8,128)S(1)} %convolution_multiply_fusion.4), channel_id=4, replica_groups=mesh['rows'=32,'chol'=16] {'rows'}, dimensions={0}, use_global_device_ids=true | all-gather | bytes 540672 | tf_op jit(solution)/shard_map/all_gather | solution.py:54
  1617.0 0.4 convolution_multiply_fusion.3
  1617.4 116.6 %all-gather.3 = f32[1024,128]{1,0:T(8,128)S(1)} all-gather(f32[32,128]{1,0:T(8,128)S(1)} %convolution_multiply_fusion.3), channel_id=5, replica_groups=mesh['rows'=32,'chol'=16] {'rows'}, dimensions={0}, use_global_device_ids=true | all-gather | bytes 540672 | tf_op jit(solution)/shard_map/all_gather | solution.py:54
  1734.0 0.4 convolution_multiply_fusion.2
  1734.4 117.3 %all-gather.4 = f32[1024,128]{1,0:T(8,128)S(1)} all-gather(f32[32,128]{1,0:T(8,128)S(1)} %convolution_multiply_fusion.2), channel_id=6, replica_groups=mesh['rows'=32,'chol'=16] {'rows'}, dimensions={0}, use_global_device_ids=true | all-gather | bytes 540672 | tf_op jit(solution)/shard_map/all_gather | solution.py:54
  1851.7 1.0 fusion.1
  (4 shorter events, 0.1 us)
Async XLA Ops:
  7.2 854.8 %copy-start = (f32[16,32768]{1,0:T(8,128)S(1)}, f32[16,32768]{1,0:T(8,128)}, u32[]{:S(2)}) copy-start(f32[16,32768]{1,0:T(8,128)} %param.6) | copy-start | bytes 6291460
  7.2 464.3 %all-reduce.3.cloned.1.call-start = ((), (), s32[]{:S(2)}) async-start(), calls=%async_computation | async-start | bytes 2097152 | tf_op jit(solution)/shard_map/psum | solution.py:24
  10.4 1248.7 %all-reduce.5.cloned.1.call-start = ((), (), s32[]{:S(2)}) async-start(), calls=%async_computation.1 | async-start | bytes 4194304 | tf_op jit(solution)/shard_map/psum | solution.py:42
  478.6 352.0 %copy-start.1 = (f32[16,128,128]{2,1,0:T(8,128)S(1)}, f32[16,128,128]{2,1,0:T(8,128)}, u32[]{:S(2)}) copy-start(f32[16,128,128]{2,1,0:T(8,128)} %all-reduce.3.cloned.1.call-done) | copy-start | bytes 3145732
  830.6 8.1 copy-start.2
  847.4 8.6 copy-start.3
  862.0 127.7 %copy-start.4 = (f32[16,16]{1,0:T(8,128)S(1)}, f32[16,16]{1,0:T(8,128)}, u32[]{:S(2)}) copy-start(f32[16,16]{1,0:T(8,128)} %param.7) | copy-start | bytes 3076
Sparse Core Ops, SparseCore 0:
  10.9 460.4 all-reduce.2
  993.0 266.0 all-reduce.4
where the time goes:
time: 1870 us; the launch traced here: 1860 us
  blocking collectives  891 us (48%)
  waiting for transfers between devices  550 us (29%)
  other arithmetic  355 us (19%)
  matrix products  45.5 us (2%)
    all_gather x6, blocking collectives, body(): lax.all_gather(term, 'rows', axis=1, tiled=True)  716 us
    psum x1, waiting for transfers between devices, body(): correlation = lax.psum(partial_correlation, 'rows')  461 us
    another operation x4, other arithmetic, body(): factor = jnp.linalg.cholesky(gram)  191 us
    another operation x3, other arithmetic, factor_solve(): lax.linalg.triangular_solve(factor, middle, left_side=True, lower=True, t...  161 us
    psum x1, blocking collectives, body(): bias = lax.psum(partial_bias, 'rows')  125 us
    psum x1, waiting for transfers between devices, body(): lax.psum(0.1 * jnp.dot(field, cholesky, precision=high, preferred_element...  88.9 us
    psum x1, blocking collectives, body(): lax.psum(jnp.sum(field * bias - 0.5 * bias * bias, axis=1), 'chol')  49.8 us
  transfers between devices with their start and end apart: 2, of which 2 were waited for; matrix products, arithmetic and copies ran while one was open for 0% of the time, Pallas kernels for 0%

commit v1 on v0

v1 whole, which is shorter than its diff:
```python
import functools

import jax
import jax.numpy as jnp
from jax import lax
from jax.experimental import pallas as pl
from jax.experimental.pallas import tpu as pltpu
from jax.sharding import PartitionSpec as P

M = 1024
NE = 128
TAYLOR = 6
NX, NZ, NH, NY, NK = 4, 8, 2, 4, 2
ROWS = NX * NZ
YK = NY * NK
BLOCK = M // ROWS
W = 16
OWN = 16
F32 = jnp.float32
BF16 = jnp.bfloat16
MESH_ID = pl.DeviceIdType.MESH
NT = (((1,), (1,)), ((), ()))
NN = (((1,), (0,)), ((), ()))
TN = (((0,), (0,)), ((), ()))


def exact(a, b, dims):
    return lax.dot_general(a, b, dims, precision=lax.Precision.HIGHEST, preferred_element_type=F32)


def split(a):
    top = a.astype(BF16)
    return top, (a - top.astype(F32)).astype(BF16)


def dot3(a, b, dims):
    def one(p, q):
        return lax.dot_general(p, q, dims, preferred_element_type=F32)

    return one(a[0], b[0]) + (one(a[0], b[1]) + one(a[1], b[0]))


def sub(index):
    return lax.broadcasted_iota(jnp.int32, index, 0)


def lane(index):
    return lax.broadcasted_iota(jnp.int32, index, 1)


def eliminate(mats):
    row8 = sub((8, NE))
    out = []
    for mat in mats:
        spread = [jnp.broadcast_to(mat[:, u : u + 1], (NE, NE)) for u in range(8)]
        small = [s[0:8] for s in spread]
        top = jnp.where(lane((8, NE)) < 8, (lane((8, NE)) == row8).astype(F32), mat[0:8])
        for t in range(8):
            inverse = 1.0 / jnp.broadcast_to(small[t][t : t + 1], (8, NE))
            pivot = small[t]
            for u in range(t + 1, 8):
                scaled = jnp.broadcast_to(small[u][t : t + 1], (8, NE)) * inverse
                small[u] = jnp.where(row8 == t, scaled, small[u] - pivot * scaled)
            scaled = jnp.broadcast_to(top[t : t + 1], (8, NE)) * inverse
            top = jnp.where(row8 == t, scaled, top - pivot * scaled)
        rest = jnp.where(lane((NE - 8, NE)) < 8, 0.0, mat[8:])
        for u in range(8):
            rest = rest - spread[u][8:] * top[u : u + 1]
        out.append(pltpu.roll(jnp.concatenate([rest, top], axis=0), NE - 8, 1))
    return tuple(out)


def kernel(
    walkers, trial, cholesky, noise, out, weight,
    slab, slab_top, slab_low, lt, cpart, crs, cag, wx, tbuf, vall, brs, pot, rc, ry, rz, px, fx, turn, lws, lwz,
    sem_l, s_c, r_c, s_a, r_a, s_w, r_w, s_t, r_t, s_v, r_v, s_b, r_b, s_k, r_k, s_y, r_y, s_z, r_z, s_p, r_p, s_f, r_f, s_l, r_l, s_m, r_m,
):
    r = lax.axis_index("rows")
    c = lax.axis_index("chol")
    x, z = r // NZ, r % NZ
    h, yk = c // YK, c % YK
    y, k = yk // NK, yk % NK

    def at(row, col):
        return (row, col)

    def row_peer(j):
        return at((r + j) % ROWS, c)

    def x_peer(j):
        return at(((x + j) % NX) * NZ + z, c)

    def z_peer(j):
        return at(x * NZ + (z + j) % NZ, c)

    def yk_peer(j):
        return at(r, h * YK + (yk + j) % YK)

    def y_peer(j):
        return at(r, h * YK + ((y + j) % NY) * NK + k)

    core_peer = at(r, h * YK + y * NK + (1 - k))
    h_peer = at(r, (1 - h) * YK + yk)

    def send(src, dst, ss, rs, dev):
        return pltpu.make_async_remote_copy(
            src_ref=src, dst_ref=dst, send_sem=ss, recv_sem=rs, device_id=dev, device_id_type=MESH_ID
        )

    def each(n, step):
        def run(j, carry):
            step(j)
            return carry

        lax.fori_loop(1, n, run, 0)

    def load(i):
        return pltpu.make_async_copy(
            cholesky.at[:, pl.ds(pl.multiple_of(i * M, M), M)], slab.at[pl.ds(pl.multiple_of(i * OWN, OWN), OWN)], sem_l.at[i]
        )

    def load_start(i, carry):
        load(i).start()
        return carry

    def load_wait(i, carry):
        load(i).wait()
        return carry

    lax.fori_loop(0, BLOCK, load_start, 0)

    barrier = pltpu.get_barrier_semaphore()

    def greet(dev):
        pl.semaphore_signal(barrier, inc=1, device_id=dev, device_id_type=MESH_ID)

    each(ROWS, lambda j: greet(row_peer(j)))
    each(YK, lambda j: greet(yk_peer(j)))
    greet(h_peer)

    own_trial = trial[pl.ds(pl.multiple_of(r * BLOCK, BLOCK), BLOCK), :]
    for s in range(NH):
        cpart[s * NE : (s + 1) * NE, :] = exact(own_trial, walkers[s * YK + yk], TN)
    wx[x] = walkers[c]

    pl.semaphore_wait(barrier, ROWS - 1 + YK - 1 + 1)

    def c_copy(j):
        part = pl.ds(pl.multiple_of(8 * ((r + j) % ROWS), 8), 8)
        return send(cpart.at[part], crs.at[j], s_c.at[j], r_c.at[j], row_peer(j))

    each(ROWS, lambda j: c_copy(j).start())

    def w_copy(j):
        return send(wx.at[x], wx.at[x], s_w.at[j], r_w.at[j], x_peer(j))

    each(NX, lambda j: w_copy(j).start())

    lax.fori_loop(0, BLOCK, load_wait, 0)
    trial_split = split(trial[...])

    def prepare(b, carry):
        rows = pl.ds(pl.multiple_of(b * 128, 128), 128)
        block = slab[rows, :]
        top, low = split(block)
        lt[rows, :] = dot3((top, low), trial_split, NN)
        for t in range(NZ):
            at_tile, at_lane = t // 4, (t % 4) * BLOCK
            pieces = [
                block[:, (2 * q + at_tile) * 128 + at_lane : (2 * q + at_tile) * 128 + at_lane + BLOCK] for q in range(NX)
            ]
            top, low = split(jnp.concatenate(pieces, axis=1))
            slab_top[rows, t * 128 : (t + 1) * 128] = top
            slab_low[rows, t * 128 : (t + 1) * 128] = low
        return carry

    lax.fori_loop(0, 4, prepare, 0)

    crs[0] = cpart[pl.ds(pl.multiple_of(8 * r, 8), 8), :]
    each(ROWS, lambda j: c_copy(j).wait_recv())
    cag[r] = jnp.sum(crs[...], axis=0)

    def a_copy(j):
        return send(cag.at[r], cag.at[r], s_a.at[j], r_a.at[j], row_peer(j))

    each(ROWS, lambda j: a_copy(j).start())

    each(NX, lambda j: w_copy(j).wait_recv())
    turn[...] = jnp.transpose(wx[...].reshape(NE, NE))
    first = turn[pl.ds(pl.multiple_of(x * BLOCK, BLOCK), BLOCK), :]
    tbuf[0, z] = first

    def t_copy(n, j):
        return send(tbuf.at[n, z], tbuf.at[n, z], s_t.at[n, j], r_t.at[n, j], z_peer(j))

    each(NZ, lambda j: t_copy(0, j).start())

    each(ROWS, lambda j: a_copy(j).wait_recv())
    both = cag[...].reshape(NH * NE, NE)
    corr = [both[s * NE : (s + 1) * NE] for s in range(NH)]
    grams = tuple(exact(m, m, TN) for m in corr)
    inverses = lax.fori_loop(0, NE // 8, lambda i, m: eliminate(m), grams)
    for s in range(NH):
        left = exact(walkers[s * YK + yk], inverses[s], NN)
        vall[yk, s] = exact(left, corr[s], NT)

    def v_copy(j):
        return send(vall.at[yk], vall.at[yk], s_v.at[j], r_v.at[j], yk_peer(j))

    each(YK, lambda j: v_copy(j).start())

    full_sub, full_lane = sub((128, 128)), lane((128, 128))
    pick_w = (sub((128, W)) // 8 == lane((128, W))).astype(F32)
    pick_g = (lane((OWN, 128)) % OWN == sub((OWN, 128))).astype(F32)
    noise_wide = exact(exact(pick_w, noise[...], NN), pick_g, NN)
    noise8 = jnp.zeros((8, 128), F32)
    for s in range(2):
        pick = (lane((8, OWN)) == sub((8, OWN)) + 8 * s).astype(F32)
        place = (lane((W, 128)) == sub((W, 128)) + W * s).astype(F32)
        noise8 = noise8 + exact(exact(pick, noise[...], NT), place, NN)
    rows512, lanes512 = sub((2 * 512, 128)), lane((2 * 512, 128))
    walker_of = ((rows512 // BLOCK) % NH) * YK + (rows512 // (BLOCK * NH)) % YK
    collect = (lanes512 == (rows512 // 512) * W + walker_of).astype(F32)
    lt_split = split(lt[...])

    each(YK, lambda j: v_copy(j).wait_recv())
    cross = dot3(lt_split, split(vall[...].reshape(512, NE)), NT)
    folded = jnp.zeros((OWN, 512), F32)
    lane_row = lane((OWN, 512)) % BLOCK
    for i in range(BLOCK):
        folded = folded + jnp.where(lane_row == i, cross[i * OWN : (i + 1) * OWN], 0.0)
    brs[r] = exact(jnp.concatenate([folded[0:8], folded[8:16]], axis=1), collect, NN)

    def b_copy(j):
        return send(brs.at[r], brs.at[r], s_b.at[j], r_b.at[j], row_peer(j))

    each(ROWS, lambda j: b_copy(j).start())
    each(ROWS, lambda j: b_copy(j).wait_recv())
    bias8 = 0.1 * jnp.sum(brs[...], axis=0)

    bias_wide = jnp.zeros((128, 128), F32)
    for s in range(2):
        pick = (full_lane == full_sub // 8 + W * s).astype(F32)
        place = (lane((8, 128)) % OWN == sub((8, 128)) + 8 * s).astype(F32)
        bias_wide = bias_wide + exact(exact(pick, bias8, NT), place, NN)
    field_wide = jnp.where(full_sub % 8 == full_lane // OWN, 0.1 * (noise_wide - bias_wide), 0.0)
    field_split = split(field_wide)
    for b in range(4):
        rows = slice(b * 128, (b + 1) * 128)
        part = dot3(field_split, (slab_top[rows, :], slab_low[rows, :]), NN)
        pot[:, b * 8 : (b + 1) * 8, :] = part.reshape(W, 8, M)

    def number(half, at_y, core):
        return half * YK + at_y * NK + core

    def k_copy(half, j):
        at_y = (y + j) % NY
        return send(
            pot.at[number(half, at_y, 1 - k)], rc.at[half, j], s_k.at[half, j], r_k.at[half, j], core_peer
        )

    def y_copy(half, j):
        return send(
            pot.at[number(half, (y + j) % NY, k)], ry.at[half, j], s_y.at[half, j], r_y.at[half, j], y_peer(j)
        )

    for half in (1 - h, h):
        each(NY, lambda j, half=half: k_copy(half, j).start())
        k_copy(half, 0).start()

    field8 = noise8 - bias8
    share = jnp.sum(field8 * bias8 - 0.5 * bias8 * bias8, axis=0, keepdims=True)
    lws[yk] = jnp.broadcast_to(share, (8, 128))

    def l_copy(j):
        return send(lws.at[yk], lws.at[yk], s_l.at[j], r_l.at[j], yk_peer(j))

    each(YK, lambda j: l_copy(j).start())

    def add_core(half, j):
        k_copy(half, j).wait_recv()
        mine = number(half, (y + j) % NY, k)
        pot[mine] = pot[mine] + rc[half, j]

    for half in (1 - h, h):

        def pass_on(j, half=half):
            add_core(half, j)
            y_copy(half, j).start()

        each(NY, pass_on)
        add_core(half, 0)

    def add_y(half):
        each(NY, lambda j: y_copy(half, j).wait_recv())
        mine = number(half, y, k)
        pot[mine] = (pot[mine] + ry[half, 1]) + (ry[half, 2] + ry[half, 3])

    add_y(1 - h)
    z_copy = send(pot.at[number(1 - h, y, k)], rz, s_z.at[0], r_z.at[0], h_peer)
    z_copy.start()
    add_y(h)

    each(YK, lambda j: l_copy(j).wait_recv())
    lwz[h] = jnp.sum(lws[...], axis=0)
    m_copy = send(lwz.at[h], lwz.at[h], s_m.at[0], r_m.at[0], h_peer)
    m_copy.start()

    z_copy.wait_recv()
    px[x] = pot[number(h, y, k)] + rz[...]

    def p_copy(j):
        return send(px.at[x], px.at[x], s_p.at[j], r_p.at[j], x_peer(j))

    each(NX, lambda j: p_copy(j).start())
    m_copy.wait_recv()
    total = lwz[0] + lwz[1]
    fold = (lane((W, 128)) % W == sub((W, 128))) & (lane((W, 128)) < 2 * W)
    weight[...] = exact(total, fold.astype(F32), NT)
    each(NX, lambda j: p_copy(j).wait_recv())
    pot_split = split(px[...].reshape(NE, M))

    sum_t = first
    for n in range(1, TAYLOR + 1):
        each(NZ, lambda j, n=n: t_copy(n - 1, j).wait_recv())
        term = jnp.concatenate([tbuf[n - 1, q] for q in range(NZ)], axis=1)
        term = dot3(split(term), pot_split, NT) / float(n)
        sum_t = sum_t + term
        if n < TAYLOR:
            tbuf[n, z] = term
            each(NZ, lambda j, n=n: t_copy(n, j).start())

    fx[x] = sum_t

    def f_copy(j):
        return send(fx.at[x], fx.at[x], s_f.at[j], r_f.at[j], x_peer(j))

    each(NX, lambda j: f_copy(j).start())

    each(ROWS, lambda j: c_copy(j).wait_send())
    each(NX, lambda j: w_copy(j).wait_send())
    each(ROWS, lambda j: a_copy(j).wait_send())
    for n in range(TAYLOR):
        each(NZ, lambda j, n=n: t_copy(n, j).wait_send())
    each(YK, lambda j: v_copy(j).wait_send())
    each(ROWS, lambda j: b_copy(j).wait_send())
    for half in (1 - h, h):
        k_copy(half, 0).wait_send()
        each(NY, lambda j, half=half: k_copy(half, j).wait_send())
        each(NY, lambda j, half=half: y_copy(half, j).wait_send())
    each(YK, lambda j: l_copy(j).wait_send())
    z_copy.wait_send()
    m_copy.wait_send()
    each(NX, lambda j: p_copy(j).wait_send())

    each(NX, lambda j: f_copy(j).wait_recv())
    turn[...] = jnp.transpose(fx[...].reshape(NE, NE))
    out[0] = turn[pl.ds(pl.multiple_of(x * BLOCK, BLOCK), BLOCK), :]
    each(NX, lambda j: f_copy(j).wait_send())


def body(walkers, trial, cholesky, noise):
    vmem = pl.BlockSpec(memory_space=pltpu.VMEM)
    dma = pltpu.SemaphoreType.DMA

    def pair(*shape):
        return [dma(shape), dma(shape)]

    propagated, weight = pl.pallas_call(
        kernel,
        name="step",
        out_shape=(jax.ShapeDtypeStruct((1, BLOCK, NE), F32), jax.ShapeDtypeStruct((8, W), F32)),
        in_specs=[vmem, vmem, pl.BlockSpec(memory_space=pl.ANY), vmem],
        out_specs=(vmem, vmem),
        scratch_shapes=[
            pltpu.VMEM((512, M), F32),
            pltpu.VMEM((512, M), BF16),
            pltpu.VMEM((512, M), BF16),
            pltpu.VMEM((512, NE), F32),
            pltpu.VMEM((NH * NE, NE), F32),
            pltpu.VMEM((ROWS, 8, NE), F32),
            pltpu.VMEM((ROWS, 8, NE), F32),
            pltpu.VMEM((NX, BLOCK, NE), F32),
            pltpu.VMEM((TAYLOR, NZ, BLOCK, NE), F32),
            pltpu.VMEM((YK, NH, BLOCK, NE), F32),
            pltpu.VMEM((ROWS, 8, 128), F32),
            pltpu.VMEM((W, BLOCK, M), F32),
            pltpu.VMEM((NH, NY, BLOCK, M), F32),
            pltpu.VMEM((NH, NY, BLOCK, M), F32),
            pltpu.VMEM((BLOCK, M), F32),
            pltpu.VMEM((NX, BLOCK, M), F32),
            pltpu.VMEM((NX, BLOCK, NE), F32),
            pltpu.VMEM((NE, NE), F32),
            pltpu.VMEM((YK, 8, 128), F32),
            pltpu.VMEM((NH, 8, 128), F32),
            dma((BLOCK,)),
            *pair(ROWS),
            *pair(ROWS),
            *pair(NX),
            *pair(TAYLOR, NZ),
            *pair(YK),
            *pair(ROWS),
            *pair(NH, NY),
            *pair(NH, NY),
            *pair(1),
            *pair(NX),
            *pair(NX),
            *pair(YK),
            *pair(1),
        ],
        compiler_params=pltpu.CompilerParams(collective_id=0, has_side_effects=True, vmem_limit_bytes=40 * 2**20),
    )(walkers, trial, cholesky, noise)
    return propagated, weight[0]


def solution(mesh):
    return jax.shard_map(
        body,
        mesh=mesh,
        in_specs=(P(None, "rows", None), P(), P("chol", "rows"), P(None, "chol")),
        out_specs=(P("chol", "rows", None), P()),
        check_vma=False,
    )
```

time: 1870 us -> 153 us (0.08)
  blocking collectives: 891 us -> 0 us
  waiting for transfers between devices: 550 us -> 0 us
  other arithmetic: 355 us -> 0 us
  Pallas kernels: 0 us -> 146 us
  matrix products: 45.5 us -> 0 us
    all_gather x6 -> x0, blocking collectives: 716 us -> none  [body(): lax.all_gather(term, 'rows', axis=1, tiled=True)]
    psum x2 -> x0, waiting for transfers between devices: 550 us -> none  [the longest x1 461 us: body(): correlation = lax.psum(partial_correlation, 'rows')]
    another operation x7 -> x0, other arithmetic: 352 us -> none  [the longest x4 191 us: body(): factor = jnp.linalg.cholesky(gram)]
    psum x2 -> x0, blocking collectives: 175 us -> none  [the longest x1 125 us: body(): bias = lax.psum(partial_bias, 'rows')]
    pallas_call x0 -> x1, Pallas kernels: none -> 146 us  [body(): pl.pallas_call(kernel, name='step', out_shape=(jax.ShapeDtypeStruct((1, B...]
    dot_general x12 -> x0, matrix products: 28.3 us -> none  [the longest x1 8.11 us: body(): right = jnp.einsum('wab,ka->wbk', correlation, trial, precision=high)]
  transfers between devices with their start and end apart: 2 -> 0, of which waited for: 2 -> 0; matrix products, arithmetic and copies ran while one was open for 0% -> 0% of each run, Pallas kernels for 0% -> 0%
where the time goes in v1:
time: 153 us; the launch traced here: 152 us
  Pallas kernels  146 us (95%)
  local copies, waits for them, and re-layouts  5.39 us (4%)
    pallas_call x1, Pallas kernels, body(): pl.pallas_call(kernel, name='step', out_shape=(jax.ShapeDtypeStruct((1, B...  146 us
    unnamed x9, local copies, waits for them, and re-layouts  4.88 us

profile of v1, /device:TPU:24, one launch (start us, length us, event | category | flops | bytes accessed | tf_op | source)
XLA Modules:
  0.0 151.8 jit_solution(14907703965062657712)
XLA Ops:
  0.6 0.0 copy-start
  0.6 1.6 %copy-done = f32[16,32768]{1,0:T(8,128)S(1)} copy-done((f32[16,32768]{1,0:T(8,128)S(1)}, f32[16,32768]{1,0:T(8,128)}, u32[]{:S(2)}) %copy-start) | copy-done | bytes 2097176
  2.2 0.0 copy-start.1
  2.2 1.0 copy-done.1
  3.3 0.0 copy-start.2
  3.3 0.9 copy-done.2
  4.2 0.0 copy-start.3
  4.2 0.7 copy-done.3
  4.9 145.7 %step.1 = (f32[1,32,128]{2,1,0:T(8,128)S(1)}, f32[8,16]{1,0:T(8,128)S(1)}) custom-call(f32[16,32,128]{2,1,0:T(8,128)S(1)} %copy-done.2, f32[1024,128]{1,0:T(8,128)S(1)} %copy-done.1, f32[16,32768]{1,0:T(8,128)S(1)} %copy-done, f32[16,16]{1,0:T(8,128)S(1)} %copy-done.3), custom_call_target="tpu_custom_call" | custom-call | tf_op jit(solution)/shard_map/step/pallas_call | solution.py:369
  150.6 0.5 slice_bitcast_fusion
  151.2 0.6 copy.7
Async XLA Ops:
  0.6 1.6 %copy-start = (f32[16,32768]{1,0:T(8,128)S(1)}, f32[16,32768]{1,0:T(8,128)}, u32[]{:S(2)}) copy-start(f32[16,32768]{1,0:T(8,128)} %cholesky.1) | copy-start | bytes 6291460
  2.2 1.0 copy-start.1
  3.3 0.9 copy-start.2
  4.2 0.7 copy-start.3

commit v2 on v1

v2 whole, which is shorter than its diff:
```python
import jax
import jax.numpy as jnp
from jax import lax
from jax.experimental import pallas as pl
from jax.experimental.pallas import tpu as pltpu
from jax.sharding import PartitionSpec as P

M = 1024
NE = 128
TAYLOR = 6
NX, NZ, NH, NY, NK = 4, 8, 2, 4, 2
ROWS = NX * NZ
YK = NY * NK
BLOCK = M // ROWS
PARTS = BLOCK // 8
W = 16
OWN = 16
F32 = jnp.float32
BF16 = jnp.bfloat16
MESH_ID = pl.DeviceIdType.MESH
NT = (((1,), (1,)), ((), ()))
NN = (((1,), (0,)), ((), ()))
TN = (((0,), (0,)), ((), ()))
STOP = 99


def exact(a, b, dims):
    return lax.dot_general(a, b, dims, precision=lax.Precision.HIGHEST, preferred_element_type=F32)


def split(a):
    top = a.astype(BF16)
    return top, (a - top.astype(F32)).astype(BF16)


def dot3(a, b, dims):
    def one(p, q):
        return lax.dot_general(p, q, dims, preferred_element_type=F32)

    return one(a[0], b[0]) + (one(a[0], b[1]) + one(a[1], b[0]))


def sub(index):
    return lax.broadcasted_iota(jnp.int32, index, 0)


def lane(index):
    return lax.broadcasted_iota(jnp.int32, index, 1)


def eliminate(mats):
    row8 = sub((8, NE))
    out = []
    for mat in mats:
        spread = [jnp.broadcast_to(mat[:, u : u + 1], (NE, NE)) for u in range(8)]
        small = [s[0:8] for s in spread]
        top = jnp.where(lane((8, NE)) < 8, (lane((8, NE)) == row8).astype(F32), mat[0:8])
        for t in range(8):
            inverse = 1.0 / jnp.broadcast_to(small[t][t : t + 1], (8, NE))
            pivot = small[t]
            for u in range(t + 1, 8):
                scaled = jnp.broadcast_to(small[u][t : t + 1], (8, NE)) * inverse
                small[u] = jnp.where(row8 == t, scaled, small[u] - pivot * scaled)
            scaled = jnp.broadcast_to(top[t : t + 1], (8, NE)) * inverse
            top = jnp.where(row8 == t, scaled, top - pivot * scaled)
        rest = jnp.where(lane((NE - 8, NE)) < 8, 0.0, mat[8:])
        for u in range(8):
            rest = rest - spread[u][8:] * top[u : u + 1]
        out.append(pltpu.roll(jnp.concatenate([rest, top], axis=0), NE - 8, 1))
    return tuple(out)


def kernel(
    walkers, trial, cholesky, noise, out, weight,
    own_w, own_t, tri, noi, slab, slab_top, slab_low, lt, cpart, crs, cag, wx, tbuf, vall, brs, pot, rc, ry, rz, px, ptop, plow, fx, turn, lws, lwz,
    sem_l, sem_i, s_c, r_c, s_a, r_a, s_w, r_w, s_t, r_t, s_v, r_v, s_b, r_b, s_k, r_k, s_y, r_y, s_z, r_z, s_p, r_p, s_f, r_f, s_l, r_l, s_m, r_m,
):
    r = lax.axis_index("rows")
    c = lax.axis_index("chol")
    x, z = r // NZ, r % NZ
    h, yk = c // YK, c % YK
    y, k = yk // NK, yk % NK
    ring = h * NZ + z
    pending = []
    owed = {}

    def place(at_x, at_z, at_h, at_yk):
        return (at_x * NZ + at_z, at_h * YK + at_yk)

    def row_peer(j):
        return ((r + j) % ROWS, c)

    def near_z(j):
        return (ring + (j + 3) % NZ - 3 + 2 * NZ) % (2 * NZ)

    def near_peer(e):
        at = near_z(e % NZ)
        return place((x + e // NZ) % NX, at % NZ, at // NZ, yk)

    def x_peer(j):
        return place((x + j) % NX, z, h, yk)

    def other_z(j):
        low = (z % 2 + j % 2) % 2
        mid = (z // 2 % 2 + j // 2 % 2) % 2
        return low + 2 * mid + 4 * ((z // 4 + j // 4) % 2)

    def z_peer(j):
        return place(x, other_z(j), h, yk)

    def yk_peer(j):
        return place(x, z, h, (yk + j) % YK)

    def y_peer(j):
        return place(x, z, h, ((y + j) % NY) * NK + k)

    core_peer = place(x, z, h, y * NK + (1 - k))
    h_peer = place(x, z, 1 - h, yk)

    def send(src, dst, ss, rs, dev):
        return pltpu.make_async_remote_copy(
            src_ref=src, dst_ref=dst, send_sem=ss, recv_sem=rs, device_id=dev, device_id_type=MESH_ID
        )

    def each(n, step, first=1):
        def run(j, carry):
            step(j)
            return carry

        lax.fori_loop(first, n, run, 0)

    def launch(name, n, copy, first=1, waits=True):
        each(n, lambda j: copy(j).start(), first)
        pending.append(lambda: each(n, lambda j: copy(j).wait_send(), first))
        owed[name] = lambda: each(n, lambda j: copy(j).wait_recv(), first)

    def arrive(name):
        owed.pop(name)()

    def finish():
        for name in list(owed):
            arrive(name)
        for wait in pending:
            wait()

    def aligned(start, size):
        return pl.ds(pl.multiple_of(start, size), size)

    def load(i):
        return pltpu.make_async_copy(
            cholesky.at[:, aligned(i * M, M)], slab.at[aligned(i * OWN, OWN)], sem_l.at[i]
        )

    first_loads = [
        pltpu.make_async_copy(trial.at[aligned(r * BLOCK, BLOCK)], own_t, sem_i.at[0]),
        pltpu.make_async_copy(walkers.at[yk], own_w.at[0], sem_i.at[1]),
        pltpu.make_async_copy(walkers.at[YK + yk], own_w.at[1], sem_i.at[2]),
    ]
    later_loads = [
        pltpu.make_async_copy(trial, tri, sem_i.at[3]),
        pltpu.make_async_copy(noise, noi, sem_i.at[4]),
        pltpu.make_async_copy(walkers.at[c], wx.at[x], sem_i.at[5]),
    ]
    for copy in first_loads:
        copy.start()

    barrier = pltpu.get_barrier_semaphore()

    def greet(dev):
        pl.semaphore_signal(barrier, inc=1, device_id=dev, device_id_type=MESH_ID)

    around = NX * 9

    def greet_near(e):
        at = (ring + e % 9 - 4 + 2 * NZ) % (2 * NZ)
        greet(place((x + e // 9) % NX, at % NZ, at // NZ, yk))

    each(4, greet_near, 0)
    each(around, greet_near, 5)
    each(YK, lambda j: greet(yk_peer(j)))
    each(BLOCK, lambda i: load(i).start(), 0)
    for copy in later_loads:
        copy.start()

    for copy in first_loads:
        copy.wait()
    for s in range(NH):
        cpart[s * NE : (s + 1) * NE, :] = exact(own_t[...], own_w[s], TN)

    pl.semaphore_wait(barrier, around - 1 + YK - 1)

    def c_copy(e):
        at = near_z(e % NZ) % NZ + NZ * ((x + e // NZ) % NX)
        return send(cpart.at[aligned(8 * at, 8)], crs.at[e], s_c.at[e], r_c.at[e], near_peer(e))

    launch("c", ROWS, c_copy)

    each(BLOCK, lambda i: load(i).wait(), 0)
    for copy in later_loads:
        copy.wait()
    trial_split = split(tri[...])

    def prepare(b):
        rows = aligned(b * 128, 128)
        block = slab[rows, :]
        top, low = split(block)
        lt[rows, :] = dot3((top, low), trial_split, NN)
        for t in range(NZ):
            at_tile, at_lane = t // 4, (t % 4) * BLOCK
            pieces = [
                block[:, (2 * q + at_tile) * 128 + at_lane : (2 * q + at_tile) * 128 + at_lane + BLOCK] for q in range(NX)
            ]
            top, low = split(jnp.concatenate(pieces, axis=1))
            slab_top[rows, t * 128 : (t + 1) * 128] = top
            slab_low[rows, t * 128 : (t + 1) * 128] = low

    each(4, prepare, 0)

    crs[0] = cpart[aligned(8 * r, 8), :]
    arrive("c")
    if STOP == 1:
        return finish()
    cag[r] = jnp.sum(crs[...], axis=0)
    launch("a", ROWS, lambda e: send(cag.at[r], cag.at[r], s_a.at[e], r_a.at[e], near_peer(e)))
    launch("w", NX, lambda j: send(wx.at[x], wx.at[x], s_w.at[j], r_w.at[j], x_peer(j)))

    full_sub, full_lane = sub((128, 128)), lane((128, 128))
    pick_w = (sub((128, W)) // 8 == lane((128, W))).astype(F32)
    pick_g = (lane((OWN, 128)) % OWN == sub((OWN, 128))).astype(F32)
    noise_wide = exact(exact(pick_w, noi[...], NN), pick_g, NN)
    own_group = lane((OWN, 128)) // W == sub((OWN, 128)) % 8
    spread_w = (lane((W, 128)) % W == sub((W, 128))).astype(F32)
    noise_rows = jnp.where(own_group, exact(noi[...], spread_w, TN), 0.0)
    noise2 = jnp.concatenate([jnp.sum(noise_rows[8 * a : 8 * a + 8], axis=0, keepdims=True) for a in range(2)], axis=0)
    rows512, lanes512 = sub((512, 128)), lane((512, 128))
    walker_of = ((rows512 // BLOCK) % NH) * YK + rows512 // (BLOCK * NH)
    collect = (lanes512 % W == walker_of).astype(F32)
    spread_g = sub((256, 128)) // 128 * 8 + (sub((256, 128)) % 128) // W == lane((256, 128)) % OWN
    spread_g = spread_g.astype(F32)
    lt_split = split(lt[...])

    arrive("w")
    turn[...] = jnp.transpose(wx[...].reshape(NE, NE))
    first = turn[aligned(x * BLOCK, BLOCK), :]
    tbuf[0, z] = first
    arrive("a")
    if STOP == 2:
        return finish()

    def t_copy(n):
        return lambda j: send(tbuf.at[n, z], tbuf.at[n, z], s_t.at[n, j], r_t.at[n, j], z_peer(j))

    launch("t0", NZ, t_copy(0))
    both = cag[...].reshape(NH * NE, NE)
    corr = [both[s * NE : (s + 1) * NE] for s in range(NH)]
    grams = tuple(exact(m, m, TN) for m in corr)
    inverses = lax.fori_loop(0, NE // 8, lambda i, m: eliminate(m), grams)
    for s in range(NH):
        left = exact(own_w[s], inverses[s], NN)
        vall[yk, s] = exact(left, corr[s], NT)
    if STOP == 3:
        return finish()
    launch("v", YK, lambda j: send(vall.at[yk], vall.at[yk], s_v.at[j], r_v.at[j], yk_peer(j)))
    arrive("v")
    if STOP == 4:
        return finish()

    cross = dot3(lt_split, split(vall[...].reshape(512, NE)), NT)
    folded = jnp.zeros((OWN, 512), F32)
    lane_row = lane((OWN, 512)) % BLOCK
    for i in range(BLOCK):
        folded = folded + jnp.where(lane_row == i, cross[i * OWN : (i + 1) * OWN], 0.0)
    share = jnp.where(own_group, exact(folded, collect, NN), 0.0)
    brs[r] = jnp.concatenate([jnp.sum(share[8 * a : 8 * a + 8], axis=0, keepdims=True) for a in range(2)], axis=0)
    launch("b", ROWS, lambda j: send(brs.at[r], brs.at[r], s_b.at[j], r_b.at[j], row_peer(j)))
    arrive("b")
    if STOP == 5:
        return finish()
    bias2 = 0.1 * jnp.sum(brs[...], axis=0)

    kept = full_lane % W == full_sub // 8
    picked = [jnp.where(kept, jnp.broadcast_to(bias2[a : a + 1], (128, 128)), 0.0) for a in range(2)]
    bias_wide = exact(jnp.concatenate(picked, axis=1), spread_g, NN)
    field_wide = jnp.where(full_sub % 8 == full_lane // OWN, 0.1 * (noise_wide - bias_wide), 0.0)
    field_split = split(field_wide)

    def number(half, at_y, core):
        return half * YK + at_y * NK + core

    def piece(ref, lead, p):
        return ref.at[(*lead, pl.ds(8 * p, 8))]

    def k_copy(half, p):
        def copy(j):
            src = piece(pot, (number(half, (y + j) % NY, 1 - k),), p)
            return send(src, piece(rc, (half, j), p), s_k.at[half, j, p], r_k.at[half, j, p], core_peer)

        return copy

    def y_copy(half, p):
        def copy(j):
            src = piece(pot, (number(half, (y + j) % NY, k),), p)
            return send(src, piece(ry, (half, j), p), s_y.at[half, j, p], r_y.at[half, j, p], y_peer(j))

        return copy

    for p in range(PARTS):
        rows = slice(p * 128, (p + 1) * 128)
        part = dot3(field_split, (slab_top[rows, :], slab_low[rows, :]), NN)
        pot[:, p * 8 : (p + 1) * 8, :] = part.reshape(W, 8, M)
        for half in (1 - h, h):
            each(NY, lambda j, half=half, p=p: k_copy(half, p)(j).start(), 0)
    for half in (1 - h, h):
        for p in range(PARTS):
            pending.append(lambda half=half, p=p: each(NY, lambda j: k_copy(half, p)(j).wait_send(), 0))

    field2 = noise2 - bias2
    lws[yk] = jnp.sum(field2 * bias2 - 0.5 * bias2 * bias2, axis=0, keepdims=True)
    launch("l", YK, lambda j: send(lws.at[yk], lws.at[yk], s_l.at[j], r_l.at[j], yk_peer(j)))

    def add_core(half, p, j):
        k_copy(half, p)(j).wait_recv()
        mine = number(half, (y + j) % NY, k)
        at = pl.ds(8 * p, 8)
        pot[mine, at] = pot[mine, at] + rc[half, j, at]

    for half in (1 - h, h):
        for p in range(PARTS):

            def pass_on(j, half=half, p=p):
                add_core(half, p, j)
                y_copy(half, p)(j).start()

            each(NY, pass_on)
            pending.append(lambda half=half, p=p: each(NY, lambda j: y_copy(half, p)(j).wait_send()))

    def add_y(half, p):
        add_core(half, p, 0)
        each(NY, lambda j: y_copy(half, p)(j).wait_recv())
        mine = number(half, y, k)
        at = pl.ds(8 * p, 8)
        pot[mine, at] = (pot[mine, at] + ry[half, 1, at]) + (ry[half, 2, at] + ry[half, 3, at])

    if STOP == 6:
        for half in (1 - h, h):
            for p in range(PARTS):
                add_y(half, p)
        return finish()

    def z_copy(p):
        src = piece(pot, (number(1 - h, y, k),), p)
        return send(src, piece(rz, (), p), s_z.at[p], r_z.at[p], h_peer)

    for p in range(PARTS):
        add_y(1 - h, p)
        z_copy(p).start()
        pending.append(lambda p=p: z_copy(p).wait_send())
    for p in range(PARTS):
        add_y(h, p)

    arrive("l")
    lwz[h] = jnp.sum(lws[...], axis=0)
    launch("m", 1, lambda j: send(lwz.at[h], lwz.at[h], s_m.at[0], r_m.at[0], h_peer), 0)

    def p_copy(p):
        def copy(j):
            ref = piece(px, (x,), p)
            return send(ref, ref, s_p.at[j, p], r_p.at[j, p], x_peer(j))

        return copy

    for p in range(PARTS):
        z_copy(p).wait_recv()
        at = slice(8 * p, 8 * p + 8)
        px[x, at] = pot[number(h, y, k), at] + rz[at]
        launch("p%d" % p, NX, p_copy(p))
    if STOP == 7:
        return finish()

    arrive("m")
    total = lwz[0] + lwz[1]
    fold = lane((W, 128)) % W == sub((W, 128))
    weight[...] = exact(jnp.broadcast_to(total, (8, 128)), fold.astype(F32), NT)[0:1]
    for p in range(PARTS):
        arrive("p%d" % p)
    if STOP == 8:
        return finish()
    pot_split = split(px[...].reshape(NE, M))
    for q in range(NZ):
        ptop[q] = pot_split[0][:, q * 128 : (q + 1) * 128]
        plow[q] = pot_split[1][:, q * 128 : (q + 1) * 128]

    sum_t = first
    for n in range(1, TAYLOR + 1):
        arrived = owed.pop("t%d" % (n - 1))
        del arrived
        term = jnp.zeros((BLOCK, NE), F32)
        for part in range(2):
            span = [other_z(4 * part + j) for j in range(4)]
            for j in range(4):
                if 4 * part + j:
                    t_copy(n - 1)(4 * part + j).wait_recv()
            held = split(jnp.concatenate([tbuf[n - 1, q] for q in span], axis=1))
            top = jnp.concatenate([ptop[q] for q in span], axis=1)
            low = jnp.concatenate([plow[q] for q in span], axis=1)
            term = term + dot3(held, (top, low), NT)
        term = term / float(n)
        sum_t = sum_t + term
        if n < TAYLOR:
            tbuf[n, z] = term
            launch("t%d" % n, NZ, lambda j, n=n: t_copy(n)((j + 2) % 7 + 1))
        if STOP == 8 + n:
            return finish()

    fx[x] = sum_t
    launch("f", NX, lambda j: send(fx.at[x], fx.at[x], s_f.at[j], r_f.at[j], x_peer(j)))
    arrive("f")
    turn[...] = jnp.transpose(fx[...].reshape(NE, NE))
    out[0] = turn[aligned(x * BLOCK, BLOCK), :]
    finish()


def call(walkers, trial, cholesky, noise, name="step", cid=0):
    vmem = pl.BlockSpec(memory_space=pltpu.VMEM)
    anywhere = pl.BlockSpec(memory_space=pl.ANY)
    dma = pltpu.SemaphoreType.DMA

    def pair(*shape):
        return [dma(shape), dma(shape)]

    propagated, weight = pl.pallas_call(
        kernel,
        name=name,
        out_shape=(jax.ShapeDtypeStruct((1, BLOCK, NE), F32), jax.ShapeDtypeStruct((1, W), F32)),
        in_specs=[anywhere] * 4,
        out_specs=(vmem, vmem),
        scratch_shapes=[
            pltpu.VMEM((NH, BLOCK, NE), F32),
            pltpu.VMEM((BLOCK, NE), F32),
            pltpu.VMEM((M, NE), F32),
            pltpu.VMEM((W, OWN), F32),
            pltpu.VMEM((512, M), F32),
            pltpu.VMEM((512, M), BF16),
            pltpu.VMEM((512, M), BF16),
            pltpu.VMEM((512, NE), F32),
            pltpu.VMEM((NH * NE, NE), F32),
            pltpu.VMEM((ROWS, 8, NE), F32),
            pltpu.VMEM((ROWS, 8, NE), F32),
            pltpu.VMEM((NX, BLOCK, NE), F32),
            pltpu.VMEM((TAYLOR, NZ, BLOCK, NE), F32),
            pltpu.VMEM((YK, NH, BLOCK, NE), F32),
            pltpu.VMEM((ROWS, 2, 128), F32),
            pltpu.VMEM((W, BLOCK, M), F32),
            pltpu.VMEM((NH, NY, BLOCK, M), F32),
            pltpu.VMEM((NH, NY, BLOCK, M), F32),
            pltpu.VMEM((BLOCK, M), F32),
            pltpu.VMEM((NX, BLOCK, M), F32),
            pltpu.VMEM((NZ, NE, 128), BF16),
            pltpu.VMEM((NZ, NE, 128), BF16),
            pltpu.VMEM((NX, BLOCK, NE), F32),
            pltpu.VMEM((NE, NE), F32),
            pltpu.VMEM((YK, 1, 128), F32),
            pltpu.VMEM((NH, 1, 128), F32),
            dma((BLOCK,)),
            dma((6,)),
            *pair(ROWS),
            *pair(ROWS),
            *pair(NX),
            *pair(TAYLOR, NZ),
            *pair(YK),
            *pair(ROWS),
            *pair(NH, NY, PARTS),
            *pair(NH, NY, PARTS),
            *pair(PARTS),
            *pair(NX, PARTS),
            *pair(NX),
            *pair(YK),
            *pair(1),
        ],
        compiler_params=pltpu.CompilerParams(collective_id=cid, has_side_effects=True, vmem_limit_bytes=60 * 2**20),
    )(walkers, trial, cholesky, noise)
    return propagated, weight.reshape(W)


def body(walkers, trial, cholesky, noise):
    return call(walkers, trial, cholesky, noise)


def solution(mesh):
    return jax.shard_map(
        body,
        mesh=mesh,
        in_specs=(P(None, "rows", None), P(), P("chol", "rows"), P(None, "chol")),
        out_specs=(P("chol", "rows", None), P()),
        check_vma=False,
    )
```

time: 153 us -> 135 us (0.88)
  Pallas kernels: 146 us -> 129 us
  local copies, waits for them, and re-layouts: 5.39 us -> 2.46 us
    pallas_call x1, Pallas kernels: 146 us -> 129 us  [call(): pl.pallas_call(kernel, name=name, out_shape=(jax.ShapeDtypeStruct((1, BLO...]
    unnamed x9 -> x2, local copies, waits for them, and re-layouts: 4.88 us -> 2.46 us
where the time goes in v2:
time: 135 us; the launch traced here: 132 us
  Pallas kernels  129 us (96%)
  local copies, waits for them, and re-layouts  2.46 us (2%)
    pallas_call x1, Pallas kernels, call(): pl.pallas_call(kernel, name=name, out_shape=(jax.ShapeDtypeStruct((1, BLO...  129 us

profile of v2, /device:TPU:24, one launch (start us, length us, event | category | flops | bytes accessed | tf_op | source)
XLA Modules:
  0.0 132.5 jit_solution(13725746393233814527)
XLA Ops:
  0.6 129.4 %step.1 = (f32[1,32,128]{2,1,0:T(8,128)}, f32[1,16]{1,0:T(1,128)}) custom-call(f32[16,32,128]{2,1,0:T(8,128)} %walkers.1, f32[1024,128]{1,0:T(8,128)} %trial.1, f32[16,32768]{1,0:T(8,128)} %cholesky.1, f32[16,16]{1,0:T(8,128)} %noise.1), custom_call_target="tpu_custom_call" | custom-call | tf_op jit(solution)/shard_map/step/pallas_call | solution.py:431
  130.0 1.3 copy.8
  131.3 1.1 copy.9

commit v3 on v2

v3 whole, which is shorter than its diff:
```python
import jax
import jax.numpy as jnp
from jax import lax
from jax.experimental import pallas as pl
from jax.experimental.pallas import tpu as pltpu
from jax.sharding import PartitionSpec as P

M = 1024
NE = 128
TAYLOR = 6
NX, NZ, NH, NY, NK = 4, 8, 2, 4, 2
ROWS = NX * NZ
YK = NY * NK
BLOCK = M // ROWS
PARTS = BLOCK // 8
W = 16
OWN = 16
F32 = jnp.float32
BF16 = jnp.bfloat16
MESH_ID = pl.DeviceIdType.MESH
NT = (((1,), (1,)), ((), ()))
NN = (((1,), (0,)), ((), ()))
TN = (((0,), (0,)), ((), ()))
AHEAD = 3
STOP = 99


def exact(a, b, dims):
    return lax.dot_general(a, b, dims, precision=lax.Precision.HIGHEST, preferred_element_type=F32)


def split(a):
    top = a.astype(BF16)
    return top, (a - top.astype(F32)).astype(BF16)


def dot3(a, b, dims):
    def one(p, q):
        return lax.dot_general(p, q, dims, preferred_element_type=F32)

    return one(a[0], b[0]) + (one(a[0], b[1]) + one(a[1], b[0]))


def sub(index):
    return lax.broadcasted_iota(jnp.int32, index, 0)


def lane(index):
    return lax.broadcasted_iota(jnp.int32, index, 1)


def pivot_block(mat, base):
    row8, lane8, lanes = sub((8, NE)), lane((8, NE)), lane((NE, NE))
    small = [jnp.broadcast_to(mat[base : base + 8, base + u : base + u + 1], (8, NE)) for u in range(8)]
    inside = (lane8 >= base) & (lane8 < base + 8)
    top = jnp.where(inside, (lane8 - base == row8).astype(F32), mat[base : base + 8])
    for t in range(8):
        inverse = 1.0 / jnp.broadcast_to(small[t][t : t + 1], (8, NE))
        pivot = small[t]
        for u in range(t + 1, 8):
            scaled = jnp.broadcast_to(small[u][t : t + 1], (8, NE)) * inverse
            small[u] = jnp.where(row8 == t, scaled, small[u] - pivot * scaled)
        scaled = jnp.broadcast_to(top[t : t + 1], (8, NE)) * inverse
        top = jnp.where(row8 == t, scaled, top - pivot * scaled)
    rest = jnp.where((lanes >= base) & (lanes < base + 8), 0.0, mat)
    rest = rest - exact(mat[:, base : base + 8], top, NN)
    above = [rest[:base]] if base else []
    return jnp.concatenate([*above, top, rest[base + 8 :]], axis=0)


def eliminate(mats):
    for q in range(4):
        mats = [pivot_block(mat, 8 * q) for mat in mats]
    return tuple(pltpu.roll(jnp.concatenate([m[32:], m[:32]], axis=0), NE - 32, 1) for m in mats)


def kernel(
    walkers, trial, cholesky, noise, out, weight,
    own_w, own_t, tri, noi, slab, slab_top, slab_low, lt, cpart, crs, cag, wz, tbuf, own_v, ball, brs, pot, rc, ry, pz, ptop, plow, fin, got, lws, lwz,
    sem_l, sem_i, s_c, r_c, s_a, r_a, s_w, r_w, s_t, r_t, s_g, r_g, s_h, r_h, s_v, r_v, s_b, r_b, s_k, r_k, s_y, r_y, s_z, r_z, s_f, r_f, s_l, r_l, s_m, r_m,
):
    r = lax.axis_index("rows")
    c = lax.axis_index("chol")
    x, z = r // NZ, r % NZ
    h, yk = c // YK, c % YK
    y, k = yk // NK, yk % NK
    ring = h * NZ + z
    goal = 2 + 4 * k
    at_goal = z == goal
    pending = []
    owed = {}

    def place(at_x, at_z, at_h, at_yk):
        return (at_x * NZ + at_z, at_h * YK + at_yk)

    def row_peer(e):
        return place((x + (e + 1) % NX) % NX, other_z(NZ - 1 - e // NX), h, yk)

    def near_z(e):
        at = e // NX
        return (ring + (1 - at % 2) * (4 - at // 2) + (at % 2) * (at // 2 - 3) + 2 * NZ) % (2 * NZ)

    def near_x(e):
        return (x + (e + 1) % NX) % NX

    def near_peer(e):
        return place(near_x(e), near_z(e) % NZ, near_z(e) // NZ, yk)

    def x_peer(j):
        return place((x + j) % NX, z, h, yk)

    def other_z(j):
        low = (z % 2 + j % 2) % 2
        mid = (z // 2 % 2 + j // 2 % 2) % 2
        return low + 2 * mid + 4 * ((z // 4 + j // 4) % 2)

    def z_peer(j):
        return place(x, other_z(j), h, yk)

    def yk_peer(j):
        return place(x, z, h, (yk + j) % YK)

    def y_peer(j):
        return place(x, z, h, ((y + j) % NY) * NK + k)

    core_peer = place(x, z, h, y * NK + (1 - k))
    h_peer = place(x, z, 1 - h, yk)

    def send(src, dst, ss, rs, dev):
        return pltpu.make_async_remote_copy(
            src_ref=src, dst_ref=dst, send_sem=ss, recv_sem=rs, device_id=dev, device_id_type=MESH_ID
        )

    def each(n, step, first=1):
        def run(j, carry):
            step(j)
            return carry

        lax.fori_loop(first, n, run, 0)

    def launch(name, n, copy, first=1, waits=True):
        each(n, lambda j: copy(j).start(), first)
        pending.append(lambda: each(n, lambda j: copy(j).wait_send(), first))
        owed[name] = lambda: each(n, lambda j: copy(j).wait_recv(), first)

    def arrive(name):
        owed.pop(name)()

    def finish():
        for name in list(owed):
            arrive(name)
        for wait in pending:
            wait()

    def aligned(start, size):
        return pl.ds(pl.multiple_of(start, size), size)

    def load(i):
        return pltpu.make_async_copy(
            cholesky.at[:, aligned(i * M, M)], slab.at[aligned(i * OWN, OWN)], sem_l.at[i]
        )

    first_loads = [
        pltpu.make_async_copy(trial.at[aligned(r * BLOCK, BLOCK)], own_t, sem_i.at[0]),
        pltpu.make_async_copy(walkers.at[yk], own_w.at[0], sem_i.at[1]),
        pltpu.make_async_copy(walkers.at[YK + yk], own_w.at[1], sem_i.at[2]),
    ]
    later_loads = [
        pltpu.make_async_copy(trial, tri, sem_i.at[3]),
        pltpu.make_async_copy(noise, noi, sem_i.at[4]),
        pltpu.make_async_copy(walkers.at[c], wz.at[z], sem_i.at[5]),
    ]
    for copy in first_loads:
        copy.start()

    barrier = pltpu.get_barrier_semaphore()

    def greet(dev):
        pl.semaphore_signal(barrier, inc=1, device_id=dev, device_id_type=MESH_ID)

    around = NX * 9

    def greet_near(e):
        at = (ring + e % 9 - 4 + 2 * NZ) % (2 * NZ)
        greet(place((x + e // 9) % NX, at % NZ, at // NZ, yk))

    each(4, greet_near, 0)
    each(around, greet_near, 5)
    each(YK, lambda j: greet(yk_peer(j)))
    each(BLOCK, lambda i: load(i).start(), 0)
    for copy in later_loads:
        copy.start()

    for copy in first_loads:
        copy.wait()
    for s in range(NH):
        cpart[s * NE : (s + 1) * NE, :] = exact(own_t[...], own_w[s], TN)

    pl.semaphore_wait(barrier, around - 1 + YK - 1)

    def c_copy(e):
        at = near_z(e) % NZ + NZ * near_x(e)
        return send(cpart.at[aligned(8 * at, 8)], crs.at[e], s_c.at[e], r_c.at[e], near_peer(e))

    launch("c", ROWS - 1, c_copy, 0)

    each(BLOCK, lambda i: load(i).wait(), 0)
    for copy in later_loads:
        copy.wait()
    trial_split = split(tri[...])

    def prepare(b):
        rows = aligned(b * 128, 128)
        block = slab[rows, :]
        top, low = split(block)
        lt[yk, rows, :] = dot3((top, low), trial_split, NN)
        slab_top[rows, :] = top
        slab_low[rows, :] = low

    each(4, prepare, 0)
    launch("g", NY, lambda j: send(lt.at[yk], lt.at[yk], s_g.at[j], r_g.at[j], y_peer(j)))

    def g_copy(j):
        ref = lt.at[(y + j) % NY * NK + k]
        return send(ref, ref, s_h.at[j], r_h.at[j], core_peer)

    launch("h0", 1, g_copy, 0)

    crs[ROWS - 1] = cpart[aligned(8 * r, 8), :]
    arrive("c")
    if STOP == 1:
        return finish()
    cag[r] = jnp.sum(crs[...], axis=0)
    launch("a", ROWS - 1, lambda e: send(cag.at[r], cag.at[r], s_a.at[e], r_a.at[e], near_peer(e)), 0)

    def w_copy(at):
        return send(wz.at[at], wz.at[at], s_w.at[0], r_w.at[at], place(x, goal, h, yk))

    @pl.when(jnp.logical_not(at_goal))
    def _():
        w_copy(z).start()

    full_sub, full_lane = sub((128, 128)), lane((128, 128))
    pick_w = (sub((128, W)) // 8 == lane((128, W))).astype(F32)
    pick_g = (lane((OWN, 128)) % OWN == sub((OWN, 128))).astype(F32)
    noise_wide = exact(exact(pick_w, noi[...], NN), pick_g, NN)
    own_g = (sub((128, 128)) // OWN == yk) & (sub((128, 128)) % OWN == lane((128, 128)) % OWN)
    own_g = own_g.astype(F32)
    same_g = (sub((128, 128)) % OWN == lane((128, 128)) % OWN).astype(F32)
    one_lane = (lane((8, 128)) < OWN).astype(F32)

    arrive("a")
    if STOP == 2:
        return finish()

    def t_copy(n):
        return lambda j: send(tbuf.at[n, x], tbuf.at[n, x], s_t.at[n, j], r_t.at[n, j], x_peer(j))

    @pl.when(at_goal)
    def _():
        each(NZ, lambda j: w_copy((z + j) % NZ).wait_recv())
        tbuf[0, x] = jnp.transpose(wz[...].reshape(NZ * BLOCK, NE))
        each(NX, lambda j: t_copy(0)(j).start())

    arrive("g")
    launch("h", NY, g_copy)
    both = cag[...].reshape(NH * NE, NE)
    corr = [both[s * NE : (s + 1) * NE] for s in range(NH)]
    grams = tuple(exact(m, m, TN) for m in corr)
    inverses = lax.fori_loop(0, NE // 32, lambda i, m: eliminate(m), grams)
    for s in range(NH):
        left = exact(own_w[s], inverses[s], NN)
        own_v[s * BLOCK : (s + 1) * BLOCK] = exact(left, corr[s], NT)
    arrive("h0")
    arrive("h")
    if STOP == 3:
        return finish()
    held_v = split(own_v[...])
    shares = []
    row_lane = lane((NH * BLOCK, 512)) // OWN == sub((NH * BLOCK, 512)) % BLOCK
    for q in range(YK):
        cross = jnp.where(row_lane, dot3(held_v, split(lt[q]), NT), 0.0)
        cross = (cross[:, 0:128] + cross[:, 128:256]) + (cross[:, 256:384] + cross[:, 384:512])
        shares.append([jnp.sum(cross[s * BLOCK : (s + 1) * BLOCK], axis=0, keepdims=True) for s in range(NH)])
    shares = jnp.concatenate([shares[q][s] for s in range(NH) for q in range(YK)], axis=0)
    shares = exact(shares, same_g, NN)
    shares = jnp.where(lane((W, 128)) // OWN == sub((W, 128)) % YK, shares, 0.0)
    brs[r] = jnp.concatenate([jnp.sum(shares[8 * a : 8 * a + 8], axis=0, keepdims=True) for a in range(2)], axis=0)
    launch("b", ROWS - 1, lambda e: send(brs.at[r], brs.at[r], s_b.at[e], r_b.at[e], row_peer(e)), 0)
    if STOP == 4:
        return finish()
    arrive("b")
    ball[yk] = 0.1 * jnp.sum(brs[...], axis=0)
    launch("v", YK, lambda j: send(ball.at[yk], ball.at[yk], s_v.at[j], r_v.at[j], yk_peer(j)))
    arrive("v")
    if STOP == 5:
        return finish()

    bias_rows = [jnp.broadcast_to(ball[q, s : s + 1], (8, 128)) for s in range(NH) for q in range(YK)]
    bias_wide = exact(jnp.concatenate(bias_rows, axis=0), own_g, NN)
    field_full = noise_wide - bias_wide
    field_wide = jnp.where(full_sub % 8 == full_lane // OWN, 0.1 * field_full, 0.0)
    field_split = split(field_wide)

    def number(half, at_y, core):
        return half * YK + at_y * NK + core

    def piece(ref, lead, p):
        return ref.at[(*lead, pl.ds(8 * p, 8))]

    def k_copy(half, p):
        def copy(j):
            src = piece(pot, (number(half, (y + j) % NY, 1 - k),), p)
            return send(src, piece(rc, (half, j), p), s_k.at[half, j, p], r_k.at[half, j, p], core_peer)

        return copy

    def y_copy(half, p):
        def copy(j):
            src = piece(pot, (number(half, (y + j) % NY, k),), p)
            return send(src, piece(ry, (half, j), p), s_y.at[half, j, p], r_y.at[half, j, p], y_peer(j))

        return copy

    for p in range(PARTS):
        rows = slice(p * 128, (p + 1) * 128)
        part = dot3(field_split, (slab_top[rows, :], slab_low[rows, :]), NN)
        pot[:, p * 8 : (p + 1) * 8, :] = part.reshape(W, 8, M)
        for half in (1 - h, h):
            each(NY, lambda j, half=half, p=p: k_copy(half, p)(j).start(), 0)
    for half in (1 - h, h):
        for p in range(PARTS):
            pending.append(lambda half=half, p=p: each(NY, lambda j: k_copy(half, p)(j).wait_send(), 0))

    exponent = field_full * bias_wide - 0.5 * bias_wide * bias_wide
    lws[yk] = exact(one_lane, exponent, NT)[0:1]
    launch("l", YK, lambda j: send(lws.at[yk], lws.at[yk], s_l.at[j], r_l.at[j], yk_peer(j)))

    def add_core(half, p, j):
        k_copy(half, p)(j).wait_recv()
        mine = number(half, (y + j) % NY, k)
        at = pl.ds(8 * p, 8)
        pot[mine, at] = pot[mine, at] + rc[half, j, at]

    def start_y(half, p):
        def pass_on(j):
            add_core(half, p, j)
            y_copy(half, p)(j).start()

        each(NY, pass_on)
        pending.append(lambda: each(NY, lambda j: y_copy(half, p)(j).wait_send()))

    def end_y(half, p):
        add_core(half, p, 0)
        each(NY, lambda j: y_copy(half, p)(j).wait_recv())
        mine = number(half, y, k)
        at = pl.ds(8 * p, 8)
        pot[mine, at] = (pot[mine, at] + ry[half, 1, at]) + (ry[half, 2, at] + ry[half, 3, at])

    def z_copy(half, p):
        src = piece(pot, (number(half, y, k),), p)
        return send(src, piece(pz, (ring,), p), s_z.at[half, p], r_z.at[ring, p], place(x, goal, half, yk))

    units = [(half, p) for p in range(PARTS) for half in (1 - h, h)]
    for unit in units[:AHEAD]:
        start_y(*unit)
    for at_unit, (half, p) in enumerate(units):
        end_y(half, p)
        if at_unit % 2 == 0:
            z_copy(half, p).start()
        else:

            @pl.when(jnp.logical_not(at_goal))
            def _(half=half, p=p):
                z_copy(half, p).start()

        if at_unit + AHEAD < len(units):
            start_y(*units[at_unit + AHEAD])

    arrive("l")
    lwz[h] = jnp.sum(lws[...], axis=0)
    launch("m", 1, lambda j: send(lwz.at[h], lwz.at[h], s_m.at[0], r_m.at[0], h_peer), 0)

    arrive("m")
    total = lwz[0] + lwz[1]
    fold = lane((W, 128)) == 8 * sub((W, 128))
    weight[...] = exact(jnp.broadcast_to(total, (8, 128)), fold.astype(F32), NT)[0:1]

    for p in range(PARTS):
        z_copy(1 - h, p).wait_send()

    @pl.when(jnp.logical_not(at_goal))
    def _():
        w_copy(z).wait_send()
        for p in range(PARTS):
            z_copy(h, p).wait_send()

    @pl.when(at_goal)
    def _():
        pz[ring] = pot[number(h, y, k)]

        def came(source, p):
            ref = piece(pz, (source,), p)
            send(ref, ref, s_z.at[0, p], r_z.at[source, p], h_peer).wait_recv()

        def assemble(j):
            row = (z + j) % NZ

            @pl.when(j > 0)
            def _():
                each(PARTS, lambda p: came(h * NZ + row, p), 0)

            each(PARTS, lambda p: came((1 - h) * NZ + row, p), 0)
            top, low = split(pz[row] + pz[NZ + row])
            rows = aligned(row * BLOCK, BLOCK)
            for q in range(NX):
                ptop[q, rows] = top[:, q * NZ * BLOCK : (q + 1) * NZ * BLOCK]
                plow[q, rows] = low[:, q * NZ * BLOCK : (q + 1) * NZ * BLOCK]

        each(NZ, assemble, 0)
        sum_t = tbuf[0, x]
        for n in range(1, TAYLOR + 1):
            term = jnp.zeros((NE, NZ * BLOCK), F32)
            if STOP >= 7 + n:
                for j in (0, 1, 3, 2):
                    if j:
                        t_copy(n - 1)(j).wait_recv()
                    at = (x + NX - j) % NX
                    term = term + dot3(split(tbuf[n - 1, at]), (ptop[at], plow[at]), NT)
                term = term / float(n)
                sum_t = sum_t + term
                if n < TAYLOR:
                    tbuf[n, x] = term
                    each(NX, lambda j, n=n: t_copy(n)(j).start())
            elif STOP == 6 + n:
                each(NX, lambda j, n=n: t_copy(n - 1)(j).wait_recv())
        fin[...] = jnp.transpose(sum_t).reshape(NZ, BLOCK, NE)

        def f_copy(j):
            return send(fin.at[(z + j) % NZ], got, s_f.at[j], r_f.at[0], place(x, (z + j) % NZ, h, yk))

        each(NZ, lambda j: f_copy(j).start())
        out[0] = fin[z]
        for n in range(min(TAYLOR, STOP - 6)):
            each(NX, lambda j, n=n: t_copy(n)(j).wait_send())
        each(NZ, lambda j: f_copy(j).wait_send())

    @pl.when(jnp.logical_not(at_goal))
    def _():
        send(fin.at[0], got, s_f.at[0], r_f.at[0], h_peer).wait_recv()
        out[0] = got[...]

    finish()


def call(walkers, trial, cholesky, noise, name="step", cid=0):
    vmem = pl.BlockSpec(memory_space=pltpu.VMEM)
    anywhere = pl.BlockSpec(memory_space=pltpu.HBM)
    dma = pltpu.SemaphoreType.DMA

    def pair(*shape):
        return [dma(shape), dma(shape)]

    propagated, weight = pl.pallas_call(
        kernel,
        name=name,
        out_shape=(jax.ShapeDtypeStruct((1, BLOCK, NE), F32), jax.ShapeDtypeStruct((1, W), F32)),
        in_specs=[anywhere] * 4,
        out_specs=(vmem, vmem),
        scratch_shapes=[
            pltpu.VMEM((NH, BLOCK, NE), F32),
            pltpu.VMEM((BLOCK, NE), F32),
            pltpu.VMEM((M, NE), F32),
            pltpu.VMEM((W, OWN), F32),
            pltpu.VMEM((512, M), F32),
            pltpu.VMEM((512, M), BF16),
            pltpu.VMEM((512, M), BF16),
            pltpu.VMEM((YK, 512, NE), F32),
            pltpu.VMEM((NH * NE, NE), F32),
            pltpu.VMEM((ROWS, 8, NE), F32),
            pltpu.VMEM((ROWS, 8, NE), F32),
            pltpu.VMEM((NZ, BLOCK, NE), F32),
            pltpu.VMEM((TAYLOR, NX, NE, NZ * BLOCK), F32),
            pltpu.VMEM((NH * BLOCK, NE), F32),
            pltpu.VMEM((YK, NH, 128), F32),
            pltpu.VMEM((ROWS, 2, 128), F32),
            pltpu.VMEM((W, BLOCK, M), F32),
            pltpu.VMEM((NH, NY, BLOCK, M), F32),
            pltpu.VMEM((NH, NY, BLOCK, M), F32),
            pltpu.VMEM((NH * NZ, BLOCK, M), F32),
            pltpu.VMEM((NX, NZ * BLOCK, NZ * BLOCK), BF16),
            pltpu.VMEM((NX, NZ * BLOCK, NZ * BLOCK), BF16),
            pltpu.VMEM((NZ, BLOCK, NE), F32),
            pltpu.VMEM((BLOCK, NE), F32),
            pltpu.VMEM((YK, 1, 128), F32),
            pltpu.VMEM((NH, 1, 128), F32),
            dma((BLOCK,)),
            dma((6,)),
            *pair(ROWS),
            *pair(ROWS),
            dma((1,)),
            dma((NZ,)),
            *pair(TAYLOR, NX),
            *pair(NY),
            *pair(NY),
            *pair(YK),
            *pair(ROWS),
            *pair(NH, NY, PARTS),
            *pair(NH, NY, PARTS),
            dma((NH, PARTS)),
            dma((NH * NZ, PARTS)),
            dma((NZ,)),
            dma((1,)),
            *pair(YK),
            *pair(1),
        ],
        compiler_params=pltpu.CompilerParams(collective_id=cid, has_side_effects=True, vmem_limit_bytes=60 * 2**20),
    )(walkers, trial, cholesky, noise)
    return propagated, weight.reshape(W)


def body(walkers, trial, cholesky, noise):
    return call(walkers, trial, cholesky, noise)


def solution(mesh):
    return jax.shard_map(
        body,
        mesh=mesh,
        in_specs=(P(None, "rows", None), P(), P("chol", "rows"), P(None, "chol")),
        out_specs=(P("chol", "rows", None), P()),
        check_vma=False,
    )
```

time: 135 us -> 126 us (0.933); the launches traced: 132 us -> 125 us
  Pallas kernels: 129 us -> 122 us
    pallas_call x1, Pallas kernels: 129 us -> 122 us  [call(): pl.pallas_call(kernel, name=name, out_shape=(jax.ShapeDtypeStruct((1, BLO...]
where the time goes in v3:
time: 126 us; the launch traced here: 125 us
  Pallas kernels  122 us (97%)
  local copies, waits for them, and re-layouts  2.46 us (2%)
    pallas_call x1, Pallas kernels, call(): pl.pallas_call(kernel, name=name, out_shape=(jax.ShapeDtypeStruct((1, BLO...  122 us

profile of v3, /device:TPU:24, one launch (start us, length us, event | category | flops | bytes accessed | tf_op | source)
XLA Modules:
  0.0 125.3 jit_solution(5324886133614321733)
XLA Ops:
  0.6 122.2 %step.1 = (f32[1,32,128]{2,1,0:T(8,128)}, f32[1,16]{1,0:T(1,128)}) custom-call(f32[16,32,128]{2,1,0:T(8,128)} %walkers.1, f32[1024,128]{1,0:T(8,128)} %trial.1, f32[16,32768]{1,0:T(8,128)} %cholesky.1, f32[16,16]{1,0:T(8,128)} %noise.1), custom_call_target="tpu_custom_call" | custom-call | tf_op jit(solution)/shard_map/step/pallas_call | solution.py:464
  122.9 1.3 %copy.8 = f32[1,32,128]{2,1,0:T(8,128)} copy(f32[1,32,128]{2,1,0:T(8,128)} %get-tuple-element.8) | data formatting | bytes 32768
  124.2 1.1 copy.9

commit v4 on v3

--- a/solution.py
+++ b/solution.py
@@ -22,6 +22,7 @@
 NN = (((1,), (0,)), ((), ()))
 TN = (((0,), (0,)), ((), ()))
 AHEAD = 3
+CHAINS = 2
 STOP = 99
 
 
@@ -253,21 +254,27 @@
     if STOP == 2:
         return finish()
 
-    def t_copy(n):
-        return lambda j: send(tbuf.at[n, x], tbuf.at[n, x], s_t.at[n, j], r_t.at[n, j], x_peer(j))
+    def t_copy(n, q):
+        def copy(j):
+            ref = tbuf.at[n, x, pl.ds(q * (NE // CHAINS), NE // CHAINS)]
+            return send(ref, ref, s_t.at[n, j, q], r_t.at[n, j, q], x_peer(j))
+
+        return copy
 
     @pl.when(at_goal)
     def _():
         each(NZ, lambda j: w_copy((z + j) % NZ).wait_recv())
         tbuf[0, x] = jnp.transpose(wz[...].reshape(NZ * BLOCK, NE))
-        each(NX, lambda j: t_copy(0)(j).start())
-
-    arrive("g")
-    launch("h", NY, g_copy)
+        for q in range(CHAINS):
+            each(NX, lambda j, q=q: t_copy(0, q)(j).start())
+
     both = cag[...].reshape(NH * NE, NE)
     corr = [both[s * NE : (s + 1) * NE] for s in range(NH)]
     grams = tuple(exact(m, m, TN) for m in corr)
-    inverses = lax.fori_loop(0, NE // 32, lambda i, m: eliminate(m), grams)
+    inverses = lax.fori_loop(0, 2, lambda i, m: eliminate(m), grams)
+    arrive("g")
+    launch("h", NY, g_copy)
+    inverses = lax.fori_loop(2, NE // 32, lambda i, m: eliminate(m), inverses)
     for s in range(NH):
         left = exact(own_w[s], inverses[s], NN)
         own_v[s * BLOCK : (s + 1) * BLOCK] = exact(left, corr[s], NT)
@@ -418,22 +425,26 @@
                 plow[q, rows] = low[:, q * NZ * BLOCK : (q + 1) * NZ * BLOCK]
 
         each(NZ, assemble, 0)
-        sum_t = tbuf[0, x]
-        for n in range(1, TAYLOR + 1):
-            term = jnp.zeros((NE, NZ * BLOCK), F32)
-            if STOP >= 7 + n:
+        span = [slice(q * (NE // CHAINS), (q + 1) * (NE // CHAINS)) for q in range(CHAINS)]
+        sums = [tbuf[0, x, span[q]] for q in range(CHAINS)]
+        for n in range(1, min(TAYLOR, STOP - 7) + 1):
+            for q in range(CHAINS):
+                term = jnp.zeros((NE // CHAINS, NZ * BLOCK), F32)
                 for j in (0, 1, 3, 2):
                     if j:
-                        t_copy(n - 1)(j).wait_recv()
+                        t_copy(n - 1, q)(j).wait_recv()
                     at = (x + NX - j) % NX
-                    term = term + dot3(split(tbuf[n - 1, at]), (ptop[at], plow[at]), NT)
+                    term = term + dot3(split(tbuf[n - 1, at, span[q]]), (ptop[at], plow[at]), NT)
                 term = term / float(n)
-                sum_t = sum_t + term
+                sums[q] = sums[q] + term
                 if n < TAYLOR:
-                    tbuf[n, x] = term
-                    each(NX, lambda j, n=n: t_copy(n)(j).start())
-            elif STOP == 6 + n:
-                each(NX, lambda j, n=n: t_copy(n - 1)(j).wait_recv())
+                    tbuf[n, x, span[q]] = term
+                    for j in (2, 1, 3):
+                        t_copy(n, q)(j).start()
+        if STOP < 7 + TAYLOR:
+            for q in range(CHAINS):
+                each(NX, lambda j, q=q: t_copy(STOP - 7, q)(j).wait_recv())
+        sum_t = jnp.concatenate(sums, axis=0)
         fin[...] = jnp.transpose(sum_t).reshape(NZ, BLOCK, NE)
 
         def f_copy(j):
@@ -442,7 +453,8 @@
         each(NZ, lambda j: f_copy(j).start())
         out[0] = fin[z]
         for n in range(min(TAYLOR, STOP - 6)):
-            each(NX, lambda j, n=n: t_copy(n)(j).wait_send())
+            for q in range(CHAINS):
+                each(NX, lambda j, n=n, q=q: t_copy(n, q)(j).wait_send())
         each(NZ, lambda j: f_copy(j).wait_send())
 
     @pl.when(jnp.logical_not(at_goal))
@@ -500,7 +512,7 @@
             *pair(ROWS),
             dma((1,)),
             dma((NZ,)),
-            *pair(TAYLOR, NX),
+            *pair(TAYLOR, NX, CHAINS),
             *pair(NY),
             *pair(NY),
             *pair(YK),

time: 126 us -> 119 us (0.944)
  Pallas kernels: 122 us -> 115 us
    pallas_call x1, Pallas kernels: 122 us -> 115 us  [call(): pl.pallas_call(kernel, name=name, out_shape=(jax.ShapeDtypeStruct((1, BLO...]
where the time goes in v4:
time: 119 us; the launch traced here: 118 us
  Pallas kernels  115 us (97%)
  local copies, waits for them, and re-layouts  2.46 us (2%)
    pallas_call x1, Pallas kernels, call(): pl.pallas_call(kernel, name=name, out_shape=(jax.ShapeDtypeStruct((1, BLO...  115 us
    unnamed x2, local copies, waits for them, and re-layouts  2.46 us

profile of v4, /device:TPU:24, one launch (start us, length us, event | category | flops | bytes accessed | tf_op | source)
XLA Modules:
  0.0 118.4 jit_solution(12622685819482043488)
XLA Ops:
  0.6 115.3 %step.1 = (f32[1,32,128]{2,1,0:T(8,128)}, f32[1,16]{1,0:T(1,128)}) custom-call(f32[16,32,128]{2,1,0:T(8,128)} %walkers.1, f32[1024,128]{1,0:T(8,128)} %trial.1, f32[16,32768]{1,0:T(8,128)} %cholesky.1, f32[16,16]{1,0:T(8,128)} %noise.1), custom_call_target="tpu_custom_call" | custom-call | tf_op jit(solution)/shard_map/step/pallas_call | solution.py:476
  115.9 1.3 %copy.8 = f32[1,32,128]{2,1,0:T(8,128)} copy(f32[1,32,128]{2,1,0:T(8,128)} %get-tuple-element.8) | data formatting | bytes 32768
  117.3 1.1 copy.9

commit v5 on v4

--- a/solution.py
+++ b/solution.py
@@ -52,9 +52,14 @@
 
 def pivot_block(mat, base):
     row8, lane8, lanes = sub((8, NE)), lane((8, NE)), lane((NE, NE))
-    small = [jnp.broadcast_to(mat[base : base + 8, base + u : base + u + 1], (8, NE)) for u in range(8)]
+
+    def spread(rows):
+        return [jnp.broadcast_to(rows[:, base + u : base + u + 1], (8, NE)) for u in range(8)]
+
+    here, after = mat[base : base + 8], mat[base + 8 : base + 16]
+    small, ahead = spread(here), spread(after)
     inside = (lane8 >= base) & (lane8 < base + 8)
-    top = jnp.where(inside, (lane8 - base == row8).astype(F32), mat[base : base + 8])
+    top = jnp.where(inside, (lane8 - base == row8).astype(F32), here)
     for t in range(8):
         inverse = 1.0 / jnp.broadcast_to(small[t][t : t + 1], (8, NE))
         pivot = small[t]
@@ -63,16 +68,20 @@
             small[u] = jnp.where(row8 == t, scaled, small[u] - pivot * scaled)
         scaled = jnp.broadcast_to(top[t : t + 1], (8, NE)) * inverse
         top = jnp.where(row8 == t, scaled, top - pivot * scaled)
-    rest = jnp.where((lanes >= base) & (lanes < base + 8), 0.0, mat)
-    rest = rest - exact(mat[:, base : base + 8], top, NN)
+    kept = jnp.where((lanes >= base) & (lanes < base + 8), 0.0, mat)
+    rest = kept - exact(mat[:, base : base + 8], top, NN)
+    part = [ahead[u] * top[u : u + 1] for u in range(8)]
+    after = kept[base + 8 : base + 16] - (
+        ((part[0] + part[1]) + (part[2] + part[3])) + ((part[4] + part[5]) + (part[6] + part[7]))
+    )
     above = [rest[:base]] if base else []
-    return jnp.concatenate([*above, top, rest[base + 8 :]], axis=0)
+    return jnp.concatenate([*above, top, after, rest[base + 16 :]], axis=0)
 
 
 def eliminate(mats):
-    for q in range(4):
+    for q in range(8):
         mats = [pivot_block(mat, 8 * q) for mat in mats]
-    return tuple(pltpu.roll(jnp.concatenate([m[32:], m[:32]], axis=0), NE - 32, 1) for m in mats)
+    return tuple(pltpu.roll(jnp.concatenate([m[64:], m[:64]], axis=0), NE - 64, 1) for m in mats)
 
 
 def kernel(
@@ -182,11 +191,11 @@
     around = NX * 9
 
     def greet_near(e):
-        at = (ring + e % 9 - 4 + 2 * NZ) % (2 * NZ)
-        greet(place((x + e // 9) % NX, at % NZ, at // NZ, yk))
-
-    each(4, greet_near, 0)
-    each(around, greet_near, 5)
+        at = e // NX
+        at = (ring + (1 - 2 * (at % 2)) * (4 - at // 2) + 2 * NZ) % (2 * NZ)
+        greet(place((x + (e + 1) % NX) % NX, at % NZ, at // NZ, yk))
+
+    each(around - 1, greet_near, 0)
     each(YK, lambda j: greet(yk_peer(j)))
     each(BLOCK, lambda i: load(i).start(), 0)
     for copy in later_loads:
@@ -271,10 +280,16 @@
     both = cag[...].reshape(NH * NE, NE)
     corr = [both[s * NE : (s + 1) * NE] for s in range(NH)]
     grams = tuple(exact(m, m, TN) for m in corr)
-    inverses = lax.fori_loop(0, 2, lambda i, m: eliminate(m), grams)
-    arrive("g")
-    launch("h", NY, g_copy)
-    inverses = lax.fori_loop(2, NE // 32, lambda i, m: eliminate(m), inverses)
+
+    def half_inverse(i, mats):
+        @pl.when(i == 1)
+        def _():
+            arrive("g")
+            launch("h", NY, g_copy)
+
+        return eliminate(mats)
+
+    inverses = lax.fori_loop(0, NE // 64, half_inverse, grams)
     for s in range(NH):
         left = exact(own_w[s], inverses[s], NN)
         own_v[s * BLOCK : (s + 1) * BLOCK] = exact(left, corr[s], NT)
@@ -329,48 +344,50 @@
 
         return copy
 
+    def add_core(half, p, j):
+        k_copy(half, p)(j).wait_recv()
+        mine = number(half, (y + j) % NY, k)
+        at = pl.ds(8 * p, 8)
+        pot[mine, at] = pot[mine, at] + rc[half, j, at]
+
+    def start_y(half, p):
+        def pass_on(j):
+            add_core(half, p, j)
+            y_copy(half, p)(j).start()
+
+        each(NY, pass_on)
+        pending.append(lambda: each(NY, lambda j: y_copy(half, p)(j).wait_send()))
+
+    def end_y(half, p):
+        add_core(half, p, 0)
+        each(NY, lambda j: y_copy(half, p)(j).wait_recv())
+        mine = number(half, y, k)
+        at = pl.ds(8 * p, 8)
+        pot[mine, at] = (pot[mine, at] + ry[half, 1, at]) + (ry[half, 2, at] + ry[half, 3, at])
+
+    def z_copy(half, p):
+        src = piece(pot, (number(half, y, k),), p)
+        return send(src, piece(pz, (ring,), p), s_z.at[half, p], r_z.at[ring, p], place(x, goal, half, yk))
+
+    units = [(half, p) for p in range(PARTS) for half in (1 - h, h)]
     for p in range(PARTS):
         rows = slice(p * 128, (p + 1) * 128)
         part = dot3(field_split, (slab_top[rows, :], slab_low[rows, :]), NN)
         pot[:, p * 8 : (p + 1) * 8, :] = part.reshape(W, 8, M)
         for half in (1 - h, h):
             each(NY, lambda j, half=half, p=p: k_copy(half, p)(j).start(), 0)
+        if p:
+            for unit in units[2 * p - 2 : min(2 * p, AHEAD)]:
+                start_y(*unit)
     for half in (1 - h, h):
         for p in range(PARTS):
             pending.append(lambda half=half, p=p: each(NY, lambda j: k_copy(half, p)(j).wait_send(), 0))
 
+
     exponent = field_full * bias_wide - 0.5 * bias_wide * bias_wide
     lws[yk] = exact(one_lane, exponent, NT)[0:1]
     launch("l", YK, lambda j: send(lws.at[yk], lws.at[yk], s_l.at[j], r_l.at[j], yk_peer(j)))
 
-    def add_core(half, p, j):
-        k_copy(half, p)(j).wait_recv()
-        mine = number(half, (y + j) % NY, k)
-        at = pl.ds(8 * p, 8)
-        pot[mine, at] = pot[mine, at] + rc[half, j, at]
-
-    def start_y(half, p):
-        def pass_on(j):
-            add_core(half, p, j)
-            y_copy(half, p)(j).start()
-
-        each(NY, pass_on)
-        pending.append(lambda: each(NY, lambda j: y_copy(half, p)(j).wait_send()))
-
-    def end_y(half, p):
-        add_core(half, p, 0)
-        each(NY, lambda j: y_copy(half, p)(j).wait_recv())
-        mine = number(half, y, k)
-        at = pl.ds(8 * p, 8)
-        pot[mine, at] = (pot[mine, at] + ry[half, 1, at]) + (ry[half, 2, at] + ry[half, 3, at])
-
-    def z_copy(half, p):
-        src = piece(pot, (number(half, y, k),), p)
-        return send(src, piece(pz, (ring,), p), s_z.at[half, p], r_z.at[ring, p], place(x, goal, half, yk))
-
-    units = [(half, p) for p in range(PARTS) for half in (1 - h, h)]
-    for unit in units[:AHEAD]:
-        start_y(*unit)
     for at_unit, (half, p) in enumerate(units):
         end_y(half, p)
         if at_unit % 2 == 0:
@@ -392,15 +409,6 @@
     total = lwz[0] + lwz[1]
     fold = lane((W, 128)) == 8 * sub((W, 128))
     weight[...] = exact(jnp.broadcast_to(total, (8, 128)), fold.astype(F32), NT)[0:1]
-
-    for p in range(PARTS):
-        z_copy(1 - h, p).wait_send()
-
-    @pl.when(jnp.logical_not(at_goal))
-    def _():
-        w_copy(z).wait_send()
-        for p in range(PARTS):
-            z_copy(h, p).wait_send()
 
     @pl.when(at_goal)
     def _():
@@ -462,7 +470,27 @@
         send(fin.at[0], got, s_f.at[0], r_f.at[0], h_peer).wait_recv()
         out[0] = got[...]
 
+    for p in range(PARTS):
+        z_copy(1 - h, p).wait_send()
+
+    @pl.when(jnp.logical_not(at_goal))
+    def _():
+        w_copy(z).wait_send()
+        for p in range(PARTS):
+            z_copy(h, p).wait_send()
+
     finish()
+
+
+def hand_over(propagated, weight, propagated_out, weight_out, sems):
+    copies = [
+        pltpu.make_async_copy(propagated, propagated_out, sems.at[0]),
+        pltpu.make_async_copy(weight.at[0], weight_out, sems.at[1]),
+    ]
+    for copy in copies:
+        copy.start()
+    for copy in copies:
+        copy.wait()
 
 
 def call(walkers, trial, cholesky, noise, name="step", cid=0):
@@ -526,9 +554,17 @@
             *pair(YK),
             *pair(1),
         ],
-        compiler_params=pltpu.CompilerParams(collective_id=cid, has_side_effects=True, vmem_limit_bytes=60 * 2**20),
+        compiler_params=pltpu.CompilerParams(collective_id=cid, has_side_effects=True, vmem_limit_bytes=215 * 2**18),
     )(walkers, trial, cholesky, noise)
-    return propagated, weight.reshape(W)
+    return pl.pallas_call(
+        hand_over,
+        name="hand_over",
+        out_shape=(jax.ShapeDtypeStruct((1, BLOCK, NE), F32), jax.ShapeDtypeStruct((W,), F32)),
+        in_specs=[pl.BlockSpec(memory_space=pl.ANY)] * 2,
+        out_specs=(pl.BlockSpec(memory_space=pl.ANY), pl.BlockSpec(memory_space=pl.ANY)),
+        scratch_shapes=[dma((2,))],
+        compiler_params=pltpu.CompilerParams(vmem_limit_bytes=2**20),
+    )(propagated, weight)
 
 
 def body(walkers, trial, cholesky, noise):

time: 119 us -> 113 us (0.950)
  Pallas kernels: 115 us -> 112 us
  local copies, waits for them, and re-layouts: 2.46 us -> 0.69 us
    pallas_call x1, Pallas kernels: 115 us -> 111 us  [call(): pl.pallas_call(kernel, name=name, out_shape=(jax.ShapeDtypeStruct((1, BLO...]
    unnamed x2, local copies, waits for them, and re-layouts: 2.46 us -> 0.69 us
where the time goes in v5:
time: 113 us
  Pallas kernels  112 us (99%)
    pallas_call x1, Pallas kernels, call(): pl.pallas_call(kernel, name=name, out_shape=(jax.ShapeDtypeStruct((1, BLO...  111 us

profile of v5, /device:TPU:24, one launch (start us, length us, event | category | flops | bytes accessed | tf_op | source)
XLA Modules:
  0.0 112.9 jit_solution(10884452909279713824)
XLA Ops:
  0.6 0.0 copy-start
  0.6 0.7 copy-done
  1.3 110.9 %step.1 = (f32[1,32,128]{2,1,0:T(8,128)S(1)}, f32[1,16]{1,0:T(1,128)S(1)}) custom-call(f32[16,32,128]{2,1,0:T(8,128)} %walkers.1, f32[1024,128]{1,0:T(8,128)} %trial.1, f32[16,32768]{1,0:T(8,128)} %cholesky.1, f32[16,16]{1,0:T(8,128)S(1)} %copy-done), custom_call_target="tpu_custom_call" | custom-call | tf_op jit(solution)/shard_map/step/pallas_call | solution.py:504
  112.2 0.6 hand_over.1
Async XLA Ops:
  0.6 0.7 copy-start

commit v6 on v5

--- a/solution.py
+++ b/solution.py
@@ -22,8 +22,7 @@
 NN = (((1,), (0,)), ((), ()))
 TN = (((0,), (0,)), ((), ()))
 AHEAD = 3
-CHAINS = 2
-STOP = 99
+CHAINS = 4
 
 
 def exact(a, b, dims):
@@ -39,7 +38,9 @@
     def one(p, q):
         return lax.dot_general(p, q, dims, preferred_element_type=F32)
 
-    return one(a[0], b[0]) + (one(a[0], b[1]) + one(a[1], b[0]))
+    rows = a[0].shape[0]
+    both = one(jnp.concatenate(a, axis=0), b[0])
+    return both[:rows] + (one(a[0], b[1]) + both[rows:])
 
 
 def sub(index):
@@ -148,10 +149,14 @@
 
         lax.fori_loop(first, n, run, 0)
 
-    def launch(name, n, copy, first=1, waits=True):
-        each(n, lambda j: copy(j).start(), first)
+    def unrolled(n, step, first=1):
+        for j in range(first, n):
+            step(j)
+
+    def launch(name, n, copy, first=1):
+        unrolled(n, lambda j: copy(j).start(), first)
         pending.append(lambda: each(n, lambda j: copy(j).wait_send(), first))
-        owed[name] = lambda: each(n, lambda j: copy(j).wait_recv(), first)
+        owed[name] = lambda: unrolled(n, lambda j: copy(j).wait_recv(), first)
 
     def arrive(name):
         owed.pop(name)()
@@ -195,17 +200,17 @@
         at = (ring + (1 - 2 * (at % 2)) * (4 - at // 2) + 2 * NZ) % (2 * NZ)
         greet(place((x + (e + 1) % NX) % NX, at % NZ, at // NZ, yk))
 
-    each(around - 1, greet_near, 0)
-    each(YK, lambda j: greet(yk_peer(j)))
-    each(BLOCK, lambda i: load(i).start(), 0)
-    for copy in later_loads:
-        copy.start()
+    unrolled(around - 1, greet_near, 0)
+    unrolled(YK, lambda j: greet(yk_peer(j)), 1)
 
     for copy in first_loads:
         copy.wait()
     for s in range(NH):
         cpart[s * NE : (s + 1) * NE, :] = exact(own_t[...], own_w[s], TN)
 
+    each(BLOCK, lambda i: load(i).start(), 0)
+    for copy in later_loads:
+        copy.start()
     pl.semaphore_wait(barrier, around - 1 + YK - 1)
 
     def c_copy(e):
@@ -238,8 +243,6 @@
 
     crs[ROWS - 1] = cpart[aligned(8 * r, 8), :]
     arrive("c")
-    if STOP == 1:
-        return finish()
     cag[r] = jnp.sum(crs[...], axis=0)
     launch("a", ROWS - 1, lambda e: send(cag.at[r], cag.at[r], s_a.at[e], r_a.at[e], near_peer(e)), 0)
 
@@ -260,8 +263,6 @@
     one_lane = (lane((8, 128)) < OWN).astype(F32)
 
     arrive("a")
-    if STOP == 2:
-        return finish()
 
     def t_copy(n, q):
         def copy(j):
@@ -295,8 +296,6 @@
         own_v[s * BLOCK : (s + 1) * BLOCK] = exact(left, corr[s], NT)
     arrive("h0")
     arrive("h")
-    if STOP == 3:
-        return finish()
     held_v = split(own_v[...])
     shares = []
     row_lane = lane((NH * BLOCK, 512)) // OWN == sub((NH * BLOCK, 512)) % BLOCK
@@ -309,14 +308,10 @@
     shares = jnp.where(lane((W, 128)) // OWN == sub((W, 128)) % YK, shares, 0.0)
     brs[r] = jnp.concatenate([jnp.sum(shares[8 * a : 8 * a + 8], axis=0, keepdims=True) for a in range(2)], axis=0)
     launch("b", ROWS - 1, lambda e: send(brs.at[r], brs.at[r], s_b.at[e], r_b.at[e], row_peer(e)), 0)
-    if STOP == 4:
-        return finish()
     arrive("b")
     ball[yk] = 0.1 * jnp.sum(brs[...], axis=0)
     launch("v", YK, lambda j: send(ball.at[yk], ball.at[yk], s_v.at[j], r_v.at[j], yk_peer(j)))
     arrive("v")
-    if STOP == 5:
-        return finish()
 
     bias_rows = [jnp.broadcast_to(ball[q, s : s + 1], (8, 128)) for s in range(NH) for q in range(YK)]
     bias_wide = exact(jnp.concatenate(bias_rows, axis=0), own_g, NN)
@@ -355,12 +350,12 @@
             add_core(half, p, j)
             y_copy(half, p)(j).start()
 
-        each(NY, pass_on)
+        unrolled(NY, pass_on, 1)
         pending.append(lambda: each(NY, lambda j: y_copy(half, p)(j).wait_send()))
 
     def end_y(half, p):
         add_core(half, p, 0)
-        each(NY, lambda j: y_copy(half, p)(j).wait_recv())
+        unrolled(NY, lambda j: y_copy(half, p)(j).wait_recv(), 1)
         mine = number(half, y, k)
         at = pl.ds(8 * p, 8)
         pot[mine, at] = (pot[mine, at] + ry[half, 1, at]) + (ry[half, 2, at] + ry[half, 3, at])
@@ -369,16 +364,17 @@
         src = piece(pot, (number(half, y, k),), p)
         return send(src, piece(pz, (ring,), p), s_z.at[half, p], r_z.at[ring, p], place(x, goal, half, yk))
 
-    units = [(half, p) for p in range(PARTS) for half in (1 - h, h)]
+    units = [(far, p) for p in range(PARTS) for far in (1, 0)]
+    side = (h, 1 - h)
     for p in range(PARTS):
         rows = slice(p * 128, (p + 1) * 128)
         part = dot3(field_split, (slab_top[rows, :], slab_low[rows, :]), NN)
         pot[:, p * 8 : (p + 1) * 8, :] = part.reshape(W, 8, M)
         for half in (1 - h, h):
-            each(NY, lambda j, half=half, p=p: k_copy(half, p)(j).start(), 0)
+            unrolled(NY, lambda j, half=half, p=p: k_copy(half, p)(j).start(), 0)
         if p:
             for unit in units[2 * p - 2 : min(2 * p, AHEAD)]:
-                start_y(*unit)
+                start_y(side[unit[0]], unit[1])
     for half in (1 - h, h):
         for p in range(PARTS):
             pending.append(lambda half=half, p=p: each(NY, lambda j: k_copy(half, p)(j).wait_send(), 0))
@@ -388,9 +384,10 @@
     lws[yk] = exact(one_lane, exponent, NT)[0:1]
     launch("l", YK, lambda j: send(lws.at[yk], lws.at[yk], s_l.at[j], r_l.at[j], yk_peer(j)))
 
-    for at_unit, (half, p) in enumerate(units):
+    for at_unit, (far, p) in enumerate(units):
+        half = side[far]
         end_y(half, p)
-        if at_unit % 2 == 0:
+        if far:
             z_copy(half, p).start()
         else:
 
@@ -399,7 +396,8 @@
                 z_copy(half, p).start()
 
         if at_unit + AHEAD < len(units):
-            start_y(*units[at_unit + AHEAD])
+            unit = units[at_unit + AHEAD]
+            start_y(side[unit[0]], unit[1])
 
     arrive("l")
     lwz[h] = jnp.sum(lws[...], axis=0)
@@ -435,7 +433,7 @@
         each(NZ, assemble, 0)
         span = [slice(q * (NE // CHAINS), (q + 1) * (NE // CHAINS)) for q in range(CHAINS)]
         sums = [tbuf[0, x, span[q]] for q in range(CHAINS)]
-        for n in range(1, min(TAYLOR, STOP - 7) + 1):
+        for n in range(1, TAYLOR + 1):
             for q in range(CHAINS):
                 term = jnp.zeros((NE // CHAINS, NZ * BLOCK), F32)
                 for j in (0, 1, 3, 2):
@@ -449,9 +447,6 @@
                     tbuf[n, x, span[q]] = term
                     for j in (2, 1, 3):
                         t_copy(n, q)(j).start()
-        if STOP < 7 + TAYLOR:
-            for q in range(CHAINS):
-                each(NX, lambda j, q=q: t_copy(STOP - 7, q)(j).wait_recv())
         sum_t = jnp.concatenate(sums, axis=0)
         fin[...] = jnp.transpose(sum_t).reshape(NZ, BLOCK, NE)
 
@@ -460,7 +455,7 @@
 
         each(NZ, lambda j: f_copy(j).start())
         out[0] = fin[z]
-        for n in range(min(TAYLOR, STOP - 6)):
+        for n in range(TAYLOR):
             for q in range(CHAINS):
                 each(NX, lambda j, n=n, q=q: t_copy(n, q)(j).wait_send())
         each(NZ, lambda j: f_copy(j).wait_send())

time: 113 us -> 109 us (0.965)
  Pallas kernels: 112 us -> 108 us
    pallas_call x1, Pallas kernels: 111 us -> 107 us  [call(): pl.pallas_call(kernel, name=name, out_shape=(jax.ShapeDtypeStruct((1, BLO...]
where the time goes in v6:
time: 109 us
  Pallas kernels  108 us (99%)
    pallas_call x1, Pallas kernels, call(): pl.pallas_call(kernel, name=name, out_shape=(jax.ShapeDtypeStruct((1, BLO...  107 us

profile of v6, /device:TPU:24, one launch (start us, length us, event | category | flops | bytes accessed | tf_op | source)
XLA Modules:
  0.0 109.1 jit_solution(13905741918510229306)
XLA Ops:
  0.6 0.0 copy-start
  0.6 0.7 copy-done
  1.3 106.9 %step.1 = (f32[1,32,128]{2,1,0:T(8,128)S(1)}, f32[1,16]{1,0:T(1,128)S(1)}) custom-call(f32[16,32,128]{2,1,0:T(8,128)} %walkers.1, f32[1024,128]{1,0:T(8,128)} %trial.1, f32[16,32768]{1,0:T(8,128)} %cholesky.1, f32[16,16]{1,0:T(8,128)S(1)} %copy-done), custom_call_target="tpu_custom_call" | custom-call | tf_op jit(solution)/shard_map/step/pallas_call | solution.py:499
  108.3 0.6 hand_over.1
Async XLA Ops:
  0.6 0.7 copy-start

commit v7 on v6

--- a/solution.py
+++ b/solution.py
@@ -434,11 +434,11 @@
         span = [slice(q * (NE // CHAINS), (q + 1) * (NE // CHAINS)) for q in range(CHAINS)]
         sums = [tbuf[0, x, span[q]] for q in range(CHAINS)]
         for n in range(1, TAYLOR + 1):
+            own = dot3(split(tbuf[n - 1, x]), (ptop[x], plow[x]), NT)
             for q in range(CHAINS):
-                term = jnp.zeros((NE // CHAINS, NZ * BLOCK), F32)
-                for j in (0, 1, 3, 2):
-                    if j:
-                        t_copy(n - 1, q)(j).wait_recv()
+                term = own[span[q]]
+                for j in (1, 3, 2):
+                    t_copy(n - 1, q)(j).wait_recv()
                     at = (x + NX - j) % NX
                     term = term + dot3(split(tbuf[n - 1, at, span[q]]), (ptop[at], plow[at]), NT)
                 term = term / float(n)

time: 109 us -> 109 us (level)
  no operation moved by 1% of the time
where the time goes in v7:
time: 109 us
  Pallas kernels  108 us (99%)
    pallas_call x1, Pallas kernels, call(): pl.pallas_call(kernel, name=name, out_shape=(jax.ShapeDtypeStruct((1, BLO...  107 us

profile of v7, /device:TPU:24, one launch (start us, length us, event | category | flops | bytes accessed | tf_op | source)
XLA Modules:
  0.0 109.0 jit_solution(3349341213121874885)
XLA Ops:
  0.6 0.0 copy-start
  0.6 0.7 copy-done
  1.3 107.0 %step.1 = (f32[1,32,128]{2,1,0:T(8,128)S(1)}, f32[1,16]{1,0:T(1,128)S(1)}) custom-call(f32[16,32,128]{2,1,0:T(8,128)} %walkers.1, f32[1024,128]{1,0:T(8,128)} %trial.1, f32[16,32768]{1,0:T(8,128)} %cholesky.1, f32[16,16]{1,0:T(8,128)S(1)} %copy-done), custom_call_target="tpu_custom_call" | custom-call | tf_op jit(solution)/shard_map/step/pallas_call | solution.py:499
  108.4 0.6 hand_over.1
Async XLA Ops:
  0.6 0.7 copy-start
